TPU v7x, 32 devices: a whole 2x2x4 slice. The times are simulated.
32 devices in a mesh: expert: 4 (over x, core), context: 4 (over z), dp: 2 (over y).
Axes of the slice: x: 2, y: 2, z: 4, core: 2. Of those that a mesh axis runs over, the one named last changes fastest.
Arguments:
- tokens: bfloat16 [4, 2048, 768], P('dp', ('expert', 'context'))
- cotangent: bfloat16 [4, 2048, 768], P('dp', ('expert', 'context')), may hold values from -6 to 6
- query_key_value_weight: bfloat16 [768, 2304], replicated, may hold values from -0.21875 to 0.21875
- output_weight: bfloat16 [768, 768], replicated, may hold values from -1.25 to 1.25
- gain_one: float32 [768], replicated, may hold values from 0.25 to 1.75
- gain_two: float32 [768], replicated, may hold values from 0.25 to 1.75
- router_weight: float32 [768, 4], replicated, may hold values from -0.15625 to 0.15625
- w_in: bfloat16 [4, 768, 3072], P('expert', None, 'context'), may hold values from -0.21875 to 0.21875
- w_down: bfloat16 [4, 768, 3072], P('expert', None, 'context'), may hold values from -0.4375 to 0.4375
- position_bias: float32 [32, 12], replicated, may hold values from -4 to 4
- bucket: int32 [4095], replicated, may hold values from 0 to 31
- route: int32 [4, 2048], P('dp', ('expert', 'context')), may hold values from 0 to 3, as said below
- slot: int32 [4, 2048], P('dp', ('expert', 'context')), may hold values from 0 to 79, as said below
- dropped: int32 [4, 2048], P('dp', ('expert', 'context')), may hold values from 0 to 1, as said below
Outputs:
- output: bfloat16 [4, 2048, 768], P('dp', ('expert', 'context'))
- d_tokens: bfloat16 [4, 2048, 768], P('dp', ('expert', 'context'))
- grad_w_qkv: float32 [768, 2304], P(('expert', 'context', 'dp'))
- grad_w_out: float32 [768, 768], P(('expert', 'context', 'dp'))
- grad_gain_one: float32 [768], P(('expert', 'context', 'dp'))
- grad_gain_two: float32 [768], P(('expert', 'context', 'dp'))
- grad_w_router: float32 [768, 4], P(('expert', 'context', 'dp'))
- grad_w_in: float32 [4, 768, 3072], P('expert', None, ('context', 'dp'))
- grad_w_down: float32 [4, 768, 3072], P('expert', None, ('context', 'dp'))
- grad_position_bias: float32 [32, 12], replicated
Inputs may be any that keep to these rules, and one draw needn't show every extreme that they name: `route`: in the 256 tokens of one device's block some expert is named by more than 80 tokens; the blocks of devices that differ only in their index of expert share that expert. Among the kept tokens of one block that name the same expert the slots are distinct; slot is 0 where dropped is 1. In each block an expert keeps at most 80 tokens, a token is dropped only where its expert keeps 80, and some expert keeps exactly 80 in every block.
All inputs are finite; a program needn't handle non-finite values.
Results may differ from a plain program's by a relative error of at most 0.02.
Values may be sent and summed in bfloat16 or wider, within the bound.
No kernel may reach another device: no remote copies, remote signals or barrier semaphores. Data moves between devices by JAX's collectives and lax.ppermute only.
A program may use at most 256 MiB of HBM per device.

v0:
```python
import jax
import jax.numpy as jnp
from jax import lax
from jax.sharding import PartitionSpec as P

D = 768
HEADS = 12
HEAD_DIM = 64


norm_epsilon = 1e-06
score_scale = 0.125
precise_mode = lax.Precision.HIGHEST
block_length = 512


def gelu_act(values):
    return jax.nn.gelu(values, approximate=True)


def offset_bias(position_bias, bucket, query_start, key_start, row_count, col_count):
    seq_len = (bucket.shape[0] + 1) // 2
    span_len = row_count + col_count - 1
    first_offset = key_start - query_start - (row_count - 1) + seq_len - 1
    picked = lax.dynamic_slice_in_dim(bucket, first_offset, span_len, 0)
    onehot = (
        picked[:, None] == jnp.arange(position_bias.shape[0], dtype=jnp.int32)[None, :]
    ).astype(jnp.float32)
    per_offset = jnp.dot(
        onehot, position_bias, precision=precise_mode, preferred_element_type=jnp.float32
    )
    head_count = per_offset.shape[1]
    padded = jnp.concatenate([per_offset.T, jnp.zeros((head_count, 1), jnp.float32)], axis=1)
    repeated = jnp.broadcast_to(padded[:, None, :], (head_count, row_count, span_len + 1))
    skewed = repeated.reshape(head_count, row_count * (span_len + 1))[:, : row_count * span_len]
    skewed = skewed.reshape(head_count, row_count, span_len)
    return (onehot, skewed[:, :, row_count - 1 : row_count - 1 + col_count])


def offset_sums(grad_block, span_len):
    head_count, row_count, col_count = grad_block.shape
    placed = jnp.pad(grad_block, ((0, 0), (0, 0), (row_count - 1, 0)))
    spread = jnp.pad(placed.reshape(head_count, row_count * span_len), ((0, 0), (0, row_count)))
    return jnp.sum(spread.reshape(head_count, row_count, span_len + 1), axis=1)[:, :span_len]


def block_scores(query_rows, key_rows, bias_rows, key_start):
    seq_count = key_rows.shape[0]
    col_count = key_rows.shape[1]
    keys_heads = key_rows.reshape(seq_count, col_count, HEADS, HEAD_DIM)
    raw_scores = jnp.einsum(
        "bqhd,bkhd->bhqk", query_rows, keys_heads, preferred_element_type=jnp.float32
    )
    bias_block = lax.dynamic_slice_in_dim(bias_rows, key_start, col_count, 2)
    return (raw_scores * score_scale + bias_block[None], keys_heads)


def over_blocks(step_fn, state_in, key_rows, value_rows):
    key_total = key_rows.shape[1]
    block_total = key_total // block_length

    def one_block(block_index, state_now):
        offset = block_index * block_length
        key_block = lax.dynamic_slice_in_dim(key_rows, offset, block_length, 1)
        value_block = lax.dynamic_slice_in_dim(value_rows, offset, block_length, 1)
        return step_fn(state_now, key_block, value_block, offset)

    return lax.fori_loop(0, block_total, one_block, state_in)


def forward_step(query_rows, bias_rows):

    def step_fn(state_now, key_rows, value_rows, key_start):
        running_max, running_sum, running_acc = state_now
        scores, keys_heads = block_scores(query_rows, key_rows, bias_rows, key_start)
        new_max = jnp.maximum(running_max, jnp.max(scores, axis=-1))
        factor = jnp.exp(running_max - new_max)
        weights = jnp.exp(scores - new_max[..., None])
        running_sum = running_sum * factor + jnp.sum(weights, axis=-1)
        values_heads = value_rows.reshape(value_rows.shape[0], value_rows.shape[1], HEADS, HEAD_DIM)
        blended = jnp.einsum(
            "bhqk,bkhd->bhqd",
            weights.astype(jnp.bfloat16),
            values_heads,
            preferred_element_type=jnp.float32,
        )
        running_acc = running_acc * factor[..., None] + blended
        return (new_max, running_sum, running_acc)

    return step_fn


def backward_step(query_rows, grad_heads, row_delta, log_total, bias_rows):

    def step_fn(state_now, key_rows, value_rows, key_start):
        grad_query, grad_keys, grad_values, grad_bias_rows = state_now
        scores, keys_heads = block_scores(query_rows, key_rows, bias_rows, key_start)
        seq_count = key_rows.shape[0]
        col_count = key_rows.shape[1]
        prob_rows = jnp.exp(scores - log_total[..., None])
        values_heads = value_rows.reshape(seq_count, col_count, HEADS, HEAD_DIM)
        grad_probs = jnp.einsum(
            "bqhd,bkhd->bhqk", grad_heads, values_heads, preferred_element_type=jnp.float32
        )
        grad_scores = (prob_rows * (grad_probs - row_delta[..., None])).astype(jnp.bfloat16)
        grad_query = grad_query + score_scale * jnp.einsum(
            "bhqk,bkhd->bqhd", grad_scores, keys_heads, preferred_element_type=jnp.float32
        )
        key_part = score_scale * jnp.einsum(
            "bhqk,bqhd->bkhd", grad_scores, query_rows, preferred_element_type=jnp.float32
        )
        value_part = jnp.einsum(
            "bhqk,bqhd->bkhd",
            prob_rows.astype(jnp.bfloat16),
            grad_heads,
            preferred_element_type=jnp.float32,
        )
        grad_keys = lax.dynamic_update_slice_in_dim(
            grad_keys, key_part.reshape(seq_count, col_count, HEADS * HEAD_DIM), key_start, 1
        )
        grad_values = lax.dynamic_update_slice_in_dim(
            grad_values, value_part.reshape(seq_count, col_count, HEADS * HEAD_DIM), key_start, 1
        )
        summed = jnp.sum(grad_scores.astype(jnp.float32), axis=0)
        grad_bias_rows = lax.dynamic_update_slice_in_dim(grad_bias_rows, summed, key_start, 2)
        return (grad_query, grad_keys, grad_values, grad_bias_rows)

    return step_fn


def contract_rows(left, right):
    return lax.dot_general(
        left, right, (((0,), (0,)), ((), ())), preferred_element_type=jnp.float32
    )


def contract_cols(left, right):
    return lax.dot_general(
        left, right, (((1,), (1,)), ((), ())), preferred_element_type=jnp.float32
    )


def exchange_back(result):
    return lax.all_to_all(result, "expert", split_axis=0, concat_axis=0, tiled=True)


def context_rows(rows_flat):
    return lax.all_gather(rows_flat, "context", axis=0, tiled=True)


def context_sum(term_fn, row_count):
    return lax.psum_scatter(
        term_fn(jnp.int32(0), row_count * lax.axis_size("context")).astype(jnp.bfloat16),
        "context",
        scatter_dimension=0,
        tiled=True,
    ).astype(jnp.float32)


def local(
    tokens,
    cotangent,
    query_key_value_weight,
    output_weight,
    gain_one,
    gain_two,
    router_weight,
    w_in,
    w_down,
    position_bias,
    bucket,
    route,
    slot,
    dropped,
):
    seq_count = tokens.shape[0]
    tok_count = tokens.shape[1]
    row_count = seq_count * tok_count
    seq_len = tok_count * lax.axis_size(("expert", "context"))
    query_start = lax.axis_index(("expert", "context")) * tok_count
    experts = lax.axis_size("expert")
    capacity = (5 * row_count + 4 * experts - 1) // (4 * experts)
    inputs = tokens.reshape(row_count, D).astype(jnp.float32)
    scale_one = lax.rsqrt(jnp.mean(inputs * inputs, axis=-1, keepdims=True) + norm_epsilon)
    normed_low = (inputs * scale_one * gain_one).astype(jnp.bfloat16)
    attention_projected = jnp.dot(
        normed_low, query_key_value_weight, preferred_element_type=jnp.float32
    ).astype(jnp.bfloat16)
    query_rows = attention_projected[:, :D].reshape(seq_count, tok_count, HEADS, HEAD_DIM)
    key_rows = attention_projected[:, D : 2 * D].reshape(seq_count, tok_count, D)
    value_rows = attention_projected[:, 2 * D :].reshape(seq_count, tok_count, D)
    onehot_all, bias_rows = offset_bias(position_bias, bucket, query_start, 0, tok_count, seq_len)
    start_stats = (
        jnp.full((seq_count, HEADS, tok_count), -jnp.inf, jnp.float32),
        jnp.zeros((seq_count, HEADS, tok_count), jnp.float32),
        jnp.zeros((seq_count, HEADS, tok_count, HEAD_DIM), jnp.float32),
    )
    forward_fn = forward_step(query_rows, bias_rows)
    pieces = (
        lax.all_gather(key_rows, ("expert", "context"), axis=1, tiled=True),
        lax.all_gather(value_rows, ("expert", "context"), axis=1, tiled=True),
    )
    running_max, running_sum, running_acc = over_blocks(
        forward_fn, start_stats, pieces[0], pieces[1]
    )
    log_total = running_max + jnp.log(running_sum)
    attended_heads = jnp.transpose(running_acc / running_sum[..., None], (0, 2, 1, 3))
    attended_low = attended_heads.reshape(row_count, D).astype(jnp.bfloat16)
    middle = inputs + jnp.dot(attended_low, output_weight, preferred_element_type=jnp.float32)
    scale_two = lax.rsqrt(jnp.mean(middle * middle, axis=-1, keepdims=True) + norm_epsilon)
    normalized_second = middle * scale_two * gain_two
    router_logits = jnp.dot(
        normalized_second, router_weight, precision=precise_mode, preferred_element_type=jnp.float32
    )
    router = jax.nn.softmax(router_logits, axis=-1)
    route_flat = route.reshape(-1)
    chosen = (route_flat[:, None] == jnp.arange(experts, dtype=jnp.int32)[None, :]).astype(
        jnp.float32
    )
    gate = jnp.sum(router * chosen, axis=-1, keepdims=True)
    sent = normalized_second.astype(jnp.bfloat16)
    position = route_flat * capacity + slot.reshape(-1)
    assign = (
        (jnp.arange(experts * capacity, dtype=jnp.int32)[:, None] == position[None, :])
        & (dropped.reshape(-1) == 0)[None, :]
    ).astype(jnp.bfloat16)
    buffer = (
        jnp.dot(assign, sent, preferred_element_type=jnp.float32)
        .astype(jnp.bfloat16)
        .reshape(experts, capacity, D)
    )
    local_in = w_in[0]
    local_down = w_down[0]
    received = lax.all_to_all(buffer, "expert", split_axis=0, concat_axis=0, tiled=True)
    source_count = received.shape[0]
    item_count = received.shape[1]
    rows_flat = received.reshape(source_count * item_count, D)
    all_rows = context_rows(rows_flat)

    def partial_out(start, count):
        hidden = gelu_act(jnp.dot(all_rows, local_in, preferred_element_type=jnp.float32)).astype(
            jnp.bfloat16
        )
        return contract_cols(hidden, local_down)

    result = context_sum(partial_out, source_count * item_count).astype(jnp.bfloat16)
    returned_buf = exchange_back(result.reshape(source_count, item_count, D))
    kept_rows = all_rows.reshape(-1, item_count, D)
    returned = contract_rows(assign, returned_buf.reshape(experts * capacity, D))
    output = (middle + gate * returned).astype(jnp.bfloat16)
    grad_out = cotangent.reshape(row_count, D).astype(jnp.float32)
    grad_gate = jnp.sum(grad_out * returned, axis=-1, keepdims=True)
    grad_returned = (gate * grad_out).astype(jnp.bfloat16)
    grad_buffer = (
        jnp.dot(assign, grad_returned, preferred_element_type=jnp.float32)
        .astype(jnp.bfloat16)
        .reshape(experts, capacity, D)
    )
    rows_grad = lax.all_to_all(
        grad_buffer, "expert", split_axis=0, concat_axis=0, tiled=True
    ).reshape(-1, D)
    rows_kept = kept_rows.reshape(-1, D)
    all_grads = context_rows(rows_grad)
    pre_act = jnp.dot(rows_kept, local_in, preferred_element_type=jnp.float32)
    hidden_value, gelu_back = jax.vjp(gelu_act, pre_act)
    hidden_low = hidden_value.astype(jnp.bfloat16)
    grad_hidden = jnp.dot(all_grads, local_down, preferred_element_type=jnp.float32)
    grad_pre = gelu_back(grad_hidden)[0].astype(jnp.bfloat16)
    down_part = contract_rows(all_grads, hidden_low)
    in_part = contract_rows(rows_kept, grad_pre)

    def partial_back(start, count):
        return contract_cols(grad_pre, local_in)

    grad_rows = context_sum(partial_back, rows_grad.shape[0]).astype(jnp.bfloat16)
    in_grad, down_grad = (
        lax.psum_scatter(
            in_part.astype(jnp.bfloat16), "dp", scatter_dimension=1, tiled=True
        ).astype(jnp.float32),
        lax.psum_scatter(
            down_part.astype(jnp.bfloat16), "dp", scatter_dimension=1, tiled=True
        ).astype(jnp.float32),
    )
    grad_back = lax.all_to_all(
        grad_rows.reshape(experts, capacity, D), "expert", split_axis=0, concat_axis=0, tiled=True
    )
    grad_sent = contract_rows(assign, grad_back.reshape(experts * capacity, D))
    grad_logits = grad_gate * gate * (chosen - router)
    router_grad = lax.dot_general(
        normalized_second,
        grad_logits,
        (((0,), (0,)), ((), ())),
        precision=precise_mode,
        preferred_element_type=jnp.float32,
    )
    grad_normed_two = grad_sent + lax.dot_general(
        grad_logits,
        router_weight,
        (((1,), (1,)), ((), ())),
        precision=precise_mode,
        preferred_element_type=jnp.float32,
    )
    scaled_two = gain_two * grad_normed_two
    cube_two = scale_two * scale_two * scale_two
    grad_middle = (
        grad_out
        + scale_two * scaled_two
        - middle * cube_two * jnp.mean(scaled_two * middle, axis=-1, keepdims=True)
    )
    gain_two_grad = jnp.sum(grad_normed_two * middle * scale_two, axis=0)
    grad_branch = grad_middle.astype(jnp.bfloat16)
    out_grad = contract_rows(attended_low, grad_branch)
    grad_heads = (
        contract_cols(grad_branch, output_weight)
        .astype(jnp.bfloat16)
        .reshape(seq_count, tok_count, HEADS, HEAD_DIM)
    )
    row_delta = jnp.einsum("bqhd,bqhd->bhq", grad_heads.astype(jnp.float32), attended_heads)
    backward_fn = backward_step(query_rows, grad_heads, row_delta, log_total, bias_rows)
    back_start = (
        jnp.zeros((seq_count, tok_count, HEADS, HEAD_DIM), jnp.float32),
        jnp.zeros((seq_count, seq_len, D), jnp.float32),
        jnp.zeros((seq_count, seq_len, D), jnp.float32),
        jnp.zeros((HEADS, tok_count, seq_len), jnp.float32),
    )
    pieces = (
        lax.all_gather(key_rows, ("expert", "context"), axis=1, tiled=True),
        lax.all_gather(value_rows, ("expert", "context"), axis=1, tiled=True),
    )
    grad_query, grad_keys_all, grad_values_all, bias_rows_grad = over_blocks(
        backward_fn, back_start, pieces[0], pieces[1]
    )
    per_offset = offset_sums(bias_rows_grad, onehot_all.shape[0])
    table_grad = jnp.dot(
        onehot_all.T, per_offset.T, precision=precise_mode, preferred_element_type=jnp.float32
    )
    grad_keys, grad_values = (
        lax.psum_scatter(
            grad_keys_all.astype(jnp.bfloat16),
            ("expert", "context"),
            scatter_dimension=1,
            tiled=True,
        ).astype(jnp.float32),
        lax.psum_scatter(
            grad_values_all.astype(jnp.bfloat16),
            ("expert", "context"),
            scatter_dimension=1,
            tiled=True,
        ).astype(jnp.float32),
    )
    grad_projected = jnp.concatenate(
        [
            grad_query.reshape(row_count, D),
            grad_keys.reshape(row_count, D),
            grad_values.reshape(row_count, D),
        ],
        axis=1,
    ).astype(jnp.bfloat16)
    qkv_grad = contract_rows(normed_low, grad_projected)
    grad_normed = contract_cols(grad_projected, query_key_value_weight)
    scaled_one = gain_one * grad_normed
    cube_one = scale_one * scale_one * scale_one
    grad_inputs = (
        grad_middle
        + scale_one * scaled_one
        - inputs * cube_one * jnp.mean(scaled_one * inputs, axis=-1, keepdims=True)
    )
    gain_one_grad = jnp.sum(grad_normed * inputs * scale_one, axis=0)
    dense = (
        lax.psum_scatter(qkv_grad, ("expert", "context", "dp"), scatter_dimension=0, tiled=True),
        lax.psum_scatter(out_grad, ("expert", "context", "dp"), scatter_dimension=0, tiled=True),
        lax.psum_scatter(
            gain_one_grad, ("expert", "context", "dp"), scatter_dimension=0, tiled=True
        ),
        lax.psum_scatter(
            gain_two_grad, ("expert", "context", "dp"), scatter_dimension=0, tiled=True
        ),
        lax.psum_scatter(router_grad, ("expert", "context", "dp"), scatter_dimension=0, tiled=True),
    )
    bias_total = lax.psum(table_grad, ("expert", "context", "dp"))
    output_rows = output.reshape(seq_count, tok_count, D)
    input_grads = grad_inputs.astype(jnp.bfloat16).reshape(seq_count, tok_count, D)
    return (
        output_rows,
        input_grads,
        dense[0],
        dense[1],
        dense[2],
        dense[3],
        dense[4],
        in_grad[None],
        down_grad[None],
        bias_total,
    )


def solution(mesh):
    placed = (
        P("dp", ("expert", "context"), None),
        P("dp", ("expert", "context"), None),
        P(),
        P(),
        P(),
        P(),
        P(),
        P("expert", None, "context"),
        P("expert", None, "context"),
        P(),
        P(),
        P("dp", ("expert", "context")),
        P("dp", ("expert", "context")),
        P("dp", ("expert", "context")),
    )
    return jax.shard_map(
        local,
        mesh=mesh,
        in_specs=placed,
        out_specs=(
            P("dp", ("expert", "context"), None),
            P("dp", ("expert", "context"), None),
            P(("expert", "context", "dp"), None),
            P(("expert", "context", "dp"), None),
            P(("expert", "context", "dp")),
            P(("expert", "context", "dp")),
            P(("expert", "context", "dp"), None),
            P("expert", None, ("context", "dp")),
            P("expert", None, ("context", "dp")),
            P(),
        ),
        check_vma=False,
    )
```

profile of v0, /device:TPU:0, one launch (start us, length us, event | category | flops | bytes accessed | tf_op | source)
XLA Modules:
  0.0 1031.6 jit_solution(11238327682363561101)
XLA Ops:
  24.9 5.7 broadcast_in_dim.73
  30.6 12.6 %pad.14 = f32[16,128,2176]{2,1,0:T(8,128)} pad(f32[12,128,2176]{2,1,0:T(8,128)} %broadcast_in_dim.73, f32[]{:T(128)} %constant.135.clone.1), padding=0_4x0_0x0_0 | pad | bytes 31195140
  43.2 16.1 %copy.140 = f32[2,8,128,2176]{3,1,2,0:T(8,128)S(1)} copy(f32[2,8,128,2176]{3,2,1,0:T(8,128)} %bitcast.233) | data formatting | bytes 35651584
  59.3 6.4 slice.26
  65.7 27.6 %reshape.229 = f32[12,128,2175]{2,1,0:T(8,128)} reshape(f32[12,278400]{1,0:T(8,128)} %slice.26) | data formatting | bytes 26726400 | tf_op jit(solution)/shard_map/reshape | solution.py:36
  93.3 12.7 %slice.27 = f32[12,128,2048]{2,1,0:T(8,128)} slice(f32[12,128,2175]{2,1,0:T(8,128)} %reshape.229), slice={[0:12], [0:128], [127:2175]} | slice | bytes 25165824 | tf_op jit(solution)/shard_map/slice | solution.py:37
  106.1 13.0 %copy.79 = f32[12,128,2048]{1,2,0:T(8,128)} copy(f32[12,128,2048]{2,1,0:T(8,128)} %slice.27) | data formatting | bytes 25165824
  121.5 28.5 %all-gather.5.cloned.1.call-done = bf16[2,2048,768]{1,2,0:T(8,128)(2,1)} async-done(((bf16[2,128,768]{1,2,0:T(8,128)(2,1)}), bf16[2,2048,768]{1,2,0:T(8,128)(2,1)}) %all-gather.5.cloned.1.call-update) | async-done | bytes 6291472 | tf_op jit(solution)/shard_map/all_gather | solution.py:200
  150.0 39.0 %while.38 = (s32[]{:T(128)}, f32[2,12,128]{2,1,0:T(8,128)S(1)}, f32[2,12,128]{2,1,0:T(8,128)}, f32[2,12,128,64]{2,3,1,0:T(8,128)}, bf16[2,2048,768]{1,2,0:T(8,12...) while((s32[]{:T(128)}, f32[2,12,128]{2,1,0:T(8,128)S(1)}, ...), condition=%wide.region_4.0_spmd.clone, body=%wide.region_1.0_spmd.clone.sunk | while | flops 420559872 | bytes 54165832 | solution.py:68
  194.1 11.6 %all_to_all.20 = bf16[4,80,768]{2,1,0:T(8,128)(2,1)} all-to-all(bf16[4,80,768]{2,1,0:T(8,128)(2,1)S(1)} %bitcast.241), channel_id=1, replica_groups=mesh['expert'=4,'context'=4,'dp'=2] {'expert'}, dimensions={0} | all-to-all | bytes 983040 | tf_op jit(solution)/shard_map/all_to_all | solution.py:234
  210.5 11.6 %all_to_all.21 = bf16[4,80,768]{2,1,0:T(8,128)(2,1)} all-to-all(bf16[4,80,768]{2,1,0:T(8,128)(2,1)S(1)} %bitcast.254), channel_id=1, replica_groups=mesh['expert'=4,'context'=4,'dp'=2] {'expert'}, dimensions={0} | all-to-all | bytes 983040 | tf_op jit(solution)/shard_map/all_to_all | solution.py:259
  222.3 25.3 %all-gather.9.cloned.1.call-done = bf16[1280,768]{1,0:T(8,128)(2,1)} async-done(((bf16[320,768]{1,0:T(8,128)(2,1)}), bf16[1280,768]{1,0:T(8,128)(2,1)}) %all-gather.9.cloned.1.call-update) | async-done | bytes 1966096 | tf_op jit(solution)/shard_map/all_gather | solution.py:148
  247.6 5.4 fusion.38
  253.1 38.4 %all-gather.11.cloned.1.call-done = bf16[1280,768]{1,0:T(8,128)(2,1)} async-done(((bf16[320,768]{1,0:T(8,128)(2,1)}), bf16[1280,768]{1,0:T(8,128)(2,1)}) %all-gather.11.cloned.1.call-update) | async-done | bytes 1966096 | tf_op jit(solution)/shard_map/all_gather | solution.py:148
  291.5 6.7 fusion.31
  299.4 3.0 convolution_convert_fusion.1
  302.5 6.2 convolution_convert_fusion.2
  308.7 34.2 %reduce-scatter.16.cloned.1.call-done = bf16[320,768]{1,0:T(8,128)(2,1)} async-done(((bf16[1280,768]{1,0:T(8,128)(2,1)}), bf16[320,768]{1,0:T(8,128)(2,1)}) %reduce-scatter.16.cloned.1.call-update) | async-done | bytes 491536 | tf_op jit(solution)/shard_map/reduce_scatter | solution.py:152
  342.9 4.1 all-to-all-start.3
  347.1 38.7 %reduce-scatter.14.cloned.1.call-done = bf16[320,768]{1,0:T(8,128)(2,1)} async-done(((bf16[1280,768]{1,0:T(8,128)(2,1)}), bf16[320,768]{1,0:T(8,128)(2,1)}) %reduce-scatter.14.cloned.1.call-update) | async-done | bytes 491536 | tf_op jit(solution)/shard_map/reduce_scatter | solution.py:152
  385.8 4.1 all-to-all-start.1
  393.7 4.8 all-to-all-done.1
  401.1 3.1 multiply_reduce_fusion.1
  416.2 3.1 broadcast.156.clone2
  419.3 3.0 broadcast.156.clone
  422.3 6.2 broadcast_in_dim.75.clone
  428.5 145.5 %while.39 = (s32[]{:T(128)}, f32[2,128,12,64]{1,3,2,0:T(8,128)}, bf16[2,2048,768]{2,1,0:T(8,128)(2,1)}, bf16[2,2048,768]{2,1,0:T(8,128)(2,1)}, f32[12,128,2048]{...) while((s32[]{:T(128)}, f32[2,128,12,64]{1,3,2,0:T(8,128)}, ...), condition=%wide.region_15.0_spmd.clone, body=%wide.region_13.15_spmd.clone.sunk | while | flops 1026883584 | bytes 121197000 | solution.py:68
  435.0 2.8 fusion.174
  437.8 4.6 convert_reduce_fusion.2
  446.0 3.5 copy.162
  452.1 4.3 convolution_multiply_fusion.3
  459.0 4.0 constant_dynamic-update-slice_fusion.6
  471.2 2.8 fusion.174
  474.0 4.6 convert_reduce_fusion.2
  482.2 3.5 copy.162
  485.7 2.6 copy.160
  488.3 4.3 convolution_multiply_fusion.3
  495.2 4.1 constant_dynamic-update-slice_fusion.6
  507.5 2.8 fusion.174
  510.3 4.6 convert_reduce_fusion.2
  518.5 3.5 copy.162
  524.7 4.3 convolution_multiply_fusion.3
  531.6 4.1 constant_dynamic-update-slice_fusion.6
  543.9 2.8 fusion.174
  546.7 4.6 convert_reduce_fusion.2
  554.9 3.5 copy.162
  561.1 4.3 convolution_multiply_fusion.3
  568.0 4.1 constant_dynamic-update-slice_fusion.6
  574.8 5.6 convolution_convert_fusion.3
  582.9 5.2 convolution_convert_fusion.4
  591.0 3.2 fusion.62
  596.7 61.0 %reduce-scatter.18.cloned.1.call-done = bf16[2,128,768]{2,1,0:T(8,128)(2,1)} async-done(((bf16[2,2048,768]{2,1,0:T(8,128)(2,1)}), bf16[2,128,768]{2,1,0:T(8,128)(2,1)}) %reduce-scatter.18.cloned.1.call-update) | async-done | bytes 393232 | tf_op jit(solution)/shard_map/reduce_scatter | solution.py:338
  659.6 86.9 %reduce-scatter.20.cloned.1.call-done = bf16[2,128,768]{2,1,0:T(8,128)(2,1)} async-done(((bf16[2,2048,768]{2,1,0:T(8,128)(2,1)}), bf16[2,128,768]{2,1,0:T(8,128)(2,1)}) %reduce-scatter.20.cloned.1.call-update) | async-done | bytes 393232 | tf_op jit(solution)/shard_map/reduce_scatter | solution.py:344
  748.5 5.4 fusion.58
  755.2 14.7 %reduce-scatter.28.cloned.1.call-done = bf16[384,768]{1,0:T(8,128)(2,1)} async-done(((bf16[768,768]{1,0:T(8,128)(2,1)}), bf16[384,768]{1,0:T(8,128)(2,1)}) %reduce-scatter.28.cloned.1.call-update) | async-done | bytes 589840
  772.0 22.4 %reduce-scatter.26.cloned.1.call-done = bf16[384,768]{1,0:T(8,128)(2,1)} async-done(((bf16[768,768]{1,0:T(8,128)(2,1)}), bf16[384,768]{1,0:T(8,128)(2,1)}) %reduce-scatter.26.cloned.1.call-update) | async-done | bytes 589840
  800.9 13.2 %pad.9.clone = f32[12,128,2175]{2,1,0:T(8,128)} pad(f32[12,128,2048]{2,1,0:T(8,128)} %get-tuple-element.359, f32[]{:T(128)} %constant.135.clone.1), padding=0_0x0_0x127_0 | pad | bytes 25946116 | tf_op jit(solution)/shard_map/jit(_pad)/pad | solution.py:42
  814.0 22.3 %reshape.246 = f32[12,278400]{1,0:T(8,128)} reshape(f32[12,128,2175]{2,1,0:T(8,128)} %pad.9.clone) | data formatting | bytes 26726400 | tf_op jit(solution)/shard_map/reshape | solution.py:43
  836.3 6.8 pad.10
  843.1 7.9 copy.143
  851.1 5.8 slice_reduce_fusion
  858.9 2.7 fusion.52
  861.6 40.5 %all-reduce.6 = (f32[768]{0:T(1024)}, f32[768]{0:T(1024)}, f32[768,4]{0,1:T(4,128)}, f32[32,12]{0,1:T(8,128)}) all-reduce(f32[768]{0:T(1024)} %get-tuple-element.508, f32[768]{0:T(1024)} %get-tuple-element.506, f32[768,4]{0,1:T(4,128)S(1)} %fusion.53, ...), channel_id=8, replica_groups=mesh['expert'=4,'context'=4,'dp'=2] {'expert','context','dp'}, use_global_device_ids=true, to_apply=%region_22.23.clone | all-reduce | flops 4992 | bytes 39936
  909.1 115.5 %reduce-scatter.22.cloned.1.call-done = f32[24,2304]{1,0:T(8,128)} async-done(((f32[768,2304]{1,0:T(8,128)}), f32[24,2304]{1,0:T(8,128)}) %reduce-scatter.22.cloned.1.call-update) | async-done | bytes 221200 | tf_op jit(solution)/shard_map/reduce_scatter | solution.py:370
  (331 shorter events, 184.6 us)
Async XLA Ops:
  7.2 3.7 copy-start
  7.2 114.3 %all-gather.7.cloned.1.call-start = ((), (), s32[]{:S(2)}) async-start(), calls=%async_computation.13 | async-start | bytes 6684672 | tf_op jit(solution)/shard_map/all_gather | solution.py:201
  15.0 135.0 %all-gather.5.cloned.1.call-start = ((), (), s32[]{:S(2)}) async-start(), calls=%async_computation.12 | async-start | bytes 6684672 | tf_op jit(solution)/shard_map/all_gather | solution.py:200
  17.0 230.6 %all-gather.9.cloned.1.call-start = ((), (), s32[]{:S(2)}) async-start(), calls=%async_computation.14 | async-start | bytes 2457600 | tf_op jit(solution)/shard_map/all_gather | solution.py:148
  152.1 2.2 copy-start.4
  161.9 2.2 copy-start.4
  171.6 2.2 copy-start.4
  189.0 4.7 copy-start.28
  189.0 4.7 copy-start.37
  189.0 4.7 copy-start.48
  190.7 15.0 %copy-start.21 = (bf16[2,128,12,64]{1,0,3,2:T(2,128)(2,1)}, bf16[2,128,12,64]{1,0,3,2:T(2,128)(2,1)S(1)}, u32[]{:S(2)}) copy-start(bf16[2,128,12,64]{1,0,3,2:T(2,128)(2,1)S(1)} %copy.80) | copy-start | bytes 1179652
  193.4 12.3 %copy-start.32 = (f32[256]{0:T(256)}, f32[256]{0:T(256)S(1)}, u32[]{:S(2)}) copy-start(f32[256]{0:T(256)S(1)} %get-tuple-element.572) | copy-start | bytes 3076
  205.7 85.7 %all-gather.11.cloned.1.call-start = ((), (), s32[]{:S(2)}) async-start(), calls=%async_computation.16 | async-start | bytes 2457600 | tf_op jit(solution)/shard_map/all_gather | solution.py:148
  209.1 13.0 %copy-start.46 = (f32[256]{0:T(256)}, f32[256]{0:T(256)S(1)}, u32[]{:S(2)}) copy-start(f32[256]{0:T(256)S(1)} %get-tuple-element.556) | copy-start | bytes 3076
  222.1 120.8 %reduce-scatter.16.cloned.1.call-start = ((), (), s32[]{:S(2)}) async-start(), calls=%async_computation.17 | async-start | bytes 2457600 | tf_op jit(solution)/shard_map/reduce_scatter | solution.py:152
  291.5 7.9 copy-start.50
  302.5 83.3 %reduce-scatter.14.cloned.1.call-start = ((), (), s32[]{:S(2)}) async-start(), calls=%async_computation.15 | async-start | bytes 2457600 | tf_op jit(solution)/shard_map/reduce_scatter | solution.py:152
  342.9 42.9 %all-to-all-start.3 = ((bf16[4,80,768]{2,1,0:T(8,128)(2,1)}), bf16[4,80,768]{2,1,0:T(8,128)(2,1)}, u32[]{:S(2)}, u32[]{:S(2)}) async-start(bf16[4,80,768]{2,1,0:T(8,128)(2,1)} %bitcast.253), calls=%async_computation.5 | async-start | bytes 983040 | tf_op jit(solution)/shard_map/all_to_all | solution.py:284
  385.8 12.7 %all-to-all-start.1 = ((bf16[4,80,768]{2,1,0:T(8,128)(2,1)}), bf16[4,80,768]{2,1,0:T(8,128)(2,1)}, u32[]{:S(2)}, u32[]{:S(2)}) async-start(bf16[4,80,768]{2,1,0:T(8,128)(2,1)} %bitcast.252), calls=%async_computation.2 | async-start | bytes 983040 | tf_op jit(solution)/shard_map/all_to_all | solution.py:144
  389.9 267.8 %reduce-scatter.18.cloned.1.call-start = ((), (), s32[]{:S(2)}) async-start(), calls=%async_computation.18 | async-start | bytes 6684672 | tf_op jit(solution)/shard_map/reduce_scatter | solution.py:338
  391.3 12.8 %copy-start.29 = (f32[768]{0:T(1024)S(1)}, f32[768]{0:T(1024)}, u32[]{:S(2)}) copy-start(f32[768]{0:T(1024)} %param.23) | copy-start | bytes 9220
  391.3 12.8 %copy-start.33 = (f32[256]{0:T(256)S(1)}, f32[256]{0:T(256)}, u32[]{:S(2)}) copy-start(f32[256]{0:T(256)} %copy-done.32) | copy-start | bytes 3076
  391.3 12.8 %copy-start.47 = (f32[256]{0:T(256)S(1)}, f32[256]{0:T(256)}, u32[]{:S(2)}) copy-start(f32[256]{0:T(256)} %copy-done.46) | copy-start | bytes 3076
  391.3 12.8 %copy-start.49 = (f32[256]{0:T(256)S(1)}, f32[256]{0:T(256)}, u32[]{:S(2)}) copy-start(f32[256]{0:T(256)} %get-tuple-element.571) | copy-start | bytes 3076
  398.5 5.7 copy-start.12
  398.5 5.7 copy-start.22
  400.3 5.9 copy-start.23
  401.1 3.1 copy-start.42
  405.3 9.1 copy-start.26
  422.3 6.2 copy-start.16
  435.0 2.8 copy-start.27
  437.8 6.3 copy-start.9
  459.0 4.0 copy-start.2
  459.0 4.0 copy-start.3
  471.2 2.8 copy-start.27
  474.0 6.3 copy-start.9
  495.2 4.1 copy-start.2
  495.2 4.1 copy-start.3
  507.5 2.8 copy-start.27
  510.3 6.3 copy-start.9
  531.6 4.1 copy-start.2
  531.6 4.1 copy-start.3
  543.9 2.8 copy-start.27
  546.7 6.3 copy-start.9
  568.0 4.1 copy-start.2
  568.0 4.1 copy-start.3
  574.0 172.5 %reduce-scatter.20.cloned.1.call-start = ((), (), s32[]{:S(2)}) async-start(), calls=%async_computation.19 | async-start | bytes 6684672 | tf_op jit(solution)/shard_map/reduce_scatter | solution.py:344
  574.8 195.1 %reduce-scatter.28.cloned.1.call-start = ((), (), s32[]{:S(2)}) async-start(), calls=%async_computation.23 | async-start | bytes 1769472
  582.9 211.5 %reduce-scatter.26.cloned.1.call-start = ((), (), s32[]{:S(2)}) async-start(), calls=%async_computation.22 | async-start | bytes 1769472
  590.6 318.6 %reduce-scatter.24.cloned.1.call-start = ((), (), s32[]{:S(2)}) async-start(), calls=%async_computation.21 | async-start | bytes 2433024 | tf_op jit(solution)/shard_map/reduce_scatter | solution.py:371
  594.2 430.4 %reduce-scatter.22.cloned.1.call-start = ((), (), s32[]{:S(2)}) async-start(), calls=%async_computation.20 | async-start | bytes 7299072 | tf_op jit(solution)/shard_map/reduce_scatter | solution.py:370
  851.0 5.9 copy-start.39
  851.0 7.2 copy-start.13
  851.0 7.2 copy-start.30
  851.0 7.2 copy-start.31
  851.0 7.2 copy-start.34
  851.0 7.1 copy-start.36
  851.0 7.1 copy-start.43
  851.0 7.8 copy-start.15
  851.1 7.8 copy-start.18
  851.1 7.8 copy-start.19
  851.1 7.8 copy-start.20
  851.1 7.8 copy-start.35
  851.1 7.8 copy-start.41
  (41 other events, 54.7 us)
Sparse Core Ops, SparseCore 0:
  15.1 68.3 all-gather.6
  86.1 63.8 all-gather.4
  205.8 41.7 all-gather.8
  249.0 42.3 all-gather.10
  302.6 40.2 reduce-scatter.15
  345.1 40.6 reduce-scatter.13
  574.2 83.5 reduce-scatter.17
  662.2 84.3 reduce-scatter.19
  748.8 21.0 reduce-scatter.27
  772.6 21.7 reduce-scatter.25
  800.3 99.0 reduce-scatter.23
  906.4 118.1 reduce-scatter.21
where the time goes:
time: 1040 us; the launch traced here: 1030 us
  waiting for transfers between devices  471 us (45%)
  local copies, waits for them, and re-layouts  306 us (29%)
  matrix products  131 us (13%)
  blocking collectives  63.7 us (6%)
  other arithmetic  34.7 us (3%)
  between operations  14.9 us (1%)
    reduce_scatter x1, waiting for transfers between devices, local(): lax.psum_scatter(qkv_grad, ('expert', 'context', 'dp'), scatter_dimension...  115 us
    reduce_scatter x1, waiting for transfers between devices, local(): lax.psum_scatter(grad_values_all.astype(jnp.bfloat16), ('expert', 'contex...  86.9 us
    reduce_scatter x2, waiting for transfers between devices, context_sum(): lax.psum_scatter(term_fn(jnp.int32(0), row_count * lax.axis_size('context...  72.9 us
    unnamed x92, local copies, waits for them, and re-layouts  71.3 us
    all_gather x2, waiting for transfers between devices, context_rows(): return lax.all_gather(rows_flat, 'context', axis=0, tiled=True)  63.7 us
    reduce_scatter x1, waiting for transfers between devices, local(): lax.psum_scatter(grad_keys_all.astype(jnp.bfloat16), ('expert', 'context'...  61 us
    unnamed x1, blocking collectives  40.5 us
    unnamed x14, waiting for transfers between devices  38 us
  transfers between devices with their start and end apart: 14, of which 11 were waited for; matrix products, arithmetic and copies ran while one was open for 23% of the time, Pallas kernels for 0%

commit v1 on v0

v1 whole, which is shorter than its diff:
```python
import functools

import jax
import jax.numpy as jnp
from jax import lax
from jax.experimental import pallas as pl
from jax.experimental.pallas import tpu as pltpu
from jax.sharding import Mesh, PartitionSpec as P

D = 768
HEADS = 12
HEAD_DIM = 64
GROUP_HEADS = 3
HEAD_GROUPS = HEADS // GROUP_HEADS
SEQ_DEV = 2
GROUPS = SEQ_DEV * HEAD_GROUPS
WIDTH = 256
SKEW = 128

norm_epsilon = 1e-06
score_scale = 0.125
precise_mode = lax.Precision.HIGHEST
vmem_bytes = 50 * 1024 * 1024
f32 = jnp.float32
bf16 = jnp.bfloat16


def matmul(left, right):
    return jnp.dot(left, right, preferred_element_type=f32)


def contract_rows(left, right):
    return lax.dot_general(left, right, (((0,), (0,)), ((), ())), preferred_element_type=f32)


def contract_cols(left, right):
    return lax.dot_general(left, right, (((1,), (1,)), ((), ())), preferred_element_type=f32)


def skewed_table(table_row):
    wide = jnp.broadcast_to(table_row, (SKEW, table_row.shape[1]))
    return pltpu.roll(wide, 1, 1, stride=1, stride_axis=0)


def forward_kernel(
    chunk, qs_ref, ks_ref, table_ref, q_ref, kv_ref, out_ref, lse_ref, skew, score, weight, rows
):
    half = table_ref.shape[2] // 2
    key_count = kv_ref.shape[2]
    skew[...] = skewed_table(table_ref[0])
    rows[...] = kv_ref[0].T
    per_chunk = chunk // WIDTH

    def one_tile(tile, carry):
        lanes = pl.ds(pl.multiple_of(tile * WIDTH, WIDTH), WIDTH)
        query = q_ref[0, :, lanes] * jnp.asarray(score_scale, bf16)
        query = jnp.concatenate([query, jnp.zeros_like(query)], axis=0)
        start = qs_ref[tile // per_chunk] + (tile % per_chunk) * WIDTH
        top = jnp.full((8, WIDTH), -jnp.inf, f32)
        for block in range(key_count // SKEW):
            offset = block * SKEW
            behind = start - ks_ref[offset // chunk] - (offset % chunk)
            bias = skew[:, pl.ds(pl.multiple_of(half + behind, SKEW), WIDTH)]
            part = matmul(rows[offset : offset + SKEW, :], query) + bias
            score[offset : offset + SKEW, :] = part
            top = jnp.maximum(top, jnp.max(part.reshape(SKEW // 8, 8, WIDTH), axis=0))
        top = jnp.max(top, axis=0, keepdims=True)
        total = jnp.zeros((8, WIDTH), f32)
        for block in range(key_count // SKEW):
            offset = block * SKEW
            part = jnp.exp(score[offset : offset + SKEW, :] - top)
            total = total + jnp.sum(part.reshape(SKEW // 8, 8, WIDTH), axis=0)
            weight[offset : offset + SKEW, :] = part.astype(bf16)
        total = jnp.sum(total, axis=0, keepdims=True)
        blended = matmul(kv_ref[0, HEAD_DIM:, :], weight[...])
        out_ref[0, :, lanes] = blended / total
        lse_ref[0, :, lanes] = top + jnp.log(total)
        return carry

    lax.fori_loop(0, q_ref.shape[2] // WIDTH, one_tile, 0)


def backward_kernel(
    chunk,
    qs_ref,
    ks_ref,
    table_ref,
    q_ref,
    kv_ref,
    out_ref,
    lse_ref,
    grad_ref,
    dq_ref,
    dkv_ref,
    dtable_ref,
    skew,
    dskew,
    rows,
    dkv,
):
    span = table_ref.shape[2]
    half = span // 2
    key_count = kv_ref.shape[2]
    skew[...] = skewed_table(table_ref[0])
    rows[...] = kv_ref[0].T
    dskew[...] = jnp.zeros_like(dskew)
    dkv[...] = jnp.zeros_like(dkv)
    per_chunk = chunk // WIDTH

    def one_tile(tile, carry):
        lanes = pl.ds(pl.multiple_of(tile * WIDTH, WIDTH), WIDTH)
        query = q_ref[0, :, lanes] * jnp.asarray(score_scale, bf16)
        grad = grad_ref[0, :, lanes]
        lse = lse_ref[0, :, lanes]
        delta = jnp.sum(grad.astype(f32) * out_ref[0, :, lanes], axis=0, keepdims=True)
        query = jnp.concatenate([query, jnp.zeros_like(query)], axis=0)
        grad = jnp.concatenate([jnp.zeros_like(grad), grad], axis=0)
        query_rows = query.T
        grad_rows = grad.T
        start = qs_ref[tile // per_chunk] + (tile % per_chunk) * WIDTH
        dq = jnp.zeros((HEAD_DIM, WIDTH), f32)
        step = 2 * SKEW
        for block in range(key_count // step):
            offset = block * step
            keys = rows[offset : offset + step, :]
            raw = matmul(keys, query)
            dprob = matmul(keys, grad)
            probs = []
            dscores = []
            for part in range(2):
                inner = offset + part * SKEW
                behind = start - ks_ref[inner // chunk] - (inner % chunk)
                here = pl.ds(pl.multiple_of(half + behind, SKEW), WIDTH)
                own = slice(part * SKEW, (part + 1) * SKEW)
                prob = jnp.exp(raw[own] + skew[:, here] - lse)
                dscore = prob * (dprob[own] - delta)
                dskew[:, here] += dscore
                probs.append(prob.astype(bf16))
                dscores.append(dscore.astype(bf16))
            prob = jnp.concatenate(probs, axis=0)
            dscore = jnp.concatenate(dscores, axis=0)
            dkv[offset : offset + step, :] += matmul(dscore, query_rows) + matmul(prob, grad_rows)
            dq = dq + matmul(kv_ref[0, :HEAD_DIM, offset : offset + step], dscore)
        dq_ref[0, :, lanes] = (dq * score_scale).astype(bf16)
        return carry

    lax.fori_loop(0, q_ref.shape[2] // WIDTH, one_tile, 0)
    dkv_ref[0] = dkv[...].T.astype(bf16)
    folded = dskew[...]
    count = SKEW
    while count > 8:
        count //= 2
        folded = folded[:count] + pltpu.roll(folded[count:], span - count, 1)
    dtable_ref[0] = folded


def head_spec(*shape):
    return pl.BlockSpec((1,) + shape, lambda head: (head, 0, 0))


def attention_forward(chunk, qs, ks, table, query, key_value):
    count, keys, span = query.shape[2], key_value.shape[2], table.shape[2]
    scalars = pl.BlockSpec(memory_space=pltpu.SMEM)
    return pl.pallas_call(
        functools.partial(forward_kernel, chunk),
        grid=(GROUP_HEADS,),
        in_specs=[
            scalars,
            scalars,
            head_spec(1, span),
            head_spec(HEAD_DIM, count),
            head_spec(2 * HEAD_DIM, keys),
        ],
        out_specs=[head_spec(HEAD_DIM, count), head_spec(1, count)],
        out_shape=[
            jax.ShapeDtypeStruct((GROUP_HEADS, HEAD_DIM, count), f32),
            jax.ShapeDtypeStruct((GROUP_HEADS, 1, count), f32),
        ],
        scratch_shapes=[
            pltpu.VMEM((SKEW, span), f32),
            pltpu.VMEM((keys, WIDTH), f32),
            pltpu.VMEM((keys, WIDTH), bf16),
            pltpu.VMEM((keys, 2 * HEAD_DIM), bf16),
        ],
        compiler_params=pltpu.CompilerParams(vmem_limit_bytes=vmem_bytes),
        cost_estimate=pl.CostEstimate(
            flops=4 * GROUP_HEADS * HEAD_DIM * count * keys * 4,
            bytes_accessed=4 * GROUP_HEADS * HEAD_DIM * (count + keys) * 2,
            transcendentals=GROUP_HEADS * count * keys,
        ),
        name="attention_forward",
    )(qs, ks, table, query, key_value)


def attention_backward(chunk, qs, ks, table, query, key_value, out, lse, grad):
    count, keys, span = query.shape[2], key_value.shape[2], table.shape[2]
    scalars = pl.BlockSpec(memory_space=pltpu.SMEM)
    return pl.pallas_call(
        functools.partial(backward_kernel, chunk),
        grid=(GROUP_HEADS,),
        in_specs=[
            scalars,
            scalars,
            head_spec(1, span),
            head_spec(HEAD_DIM, count),
            head_spec(2 * HEAD_DIM, keys),
            head_spec(HEAD_DIM, count),
            head_spec(1, count),
            head_spec(HEAD_DIM, count),
        ],
        out_specs=[
            head_spec(HEAD_DIM, count),
            head_spec(2 * HEAD_DIM, keys),
            head_spec(8, span),
        ],
        out_shape=[
            jax.ShapeDtypeStruct((GROUP_HEADS, HEAD_DIM, count), bf16),
            jax.ShapeDtypeStruct((GROUP_HEADS, 2 * HEAD_DIM, keys), bf16),
            jax.ShapeDtypeStruct((GROUP_HEADS, 8, span), f32),
        ],
        scratch_shapes=[
            pltpu.VMEM((SKEW, span), f32),
            pltpu.VMEM((SKEW, span), f32),
            pltpu.VMEM((keys, 2 * HEAD_DIM), bf16),
            pltpu.VMEM((keys, 2 * HEAD_DIM), f32),
        ],
        compiler_params=pltpu.CompilerParams(vmem_limit_bytes=vmem_bytes),
        cost_estimate=pl.CostEstimate(
            flops=10 * GROUP_HEADS * HEAD_DIM * count * keys * 4,
            bytes_accessed=4 * GROUP_HEADS * HEAD_DIM * (count + keys) * 4,
            transcendentals=GROUP_HEADS * count * keys,
        ),
        name="attention_backward",
    )(qs, ks, table, query, key_value, out, lse, grad)


def shift(value, axis, step):
    size = lax.axis_size(axis)
    return lax.ppermute(value, axis, [(i, (i + step) % size) for i in range(size)])


def pick(value, index, dim=0):
    return lax.dynamic_index_in_dim(value, index, dim, keepdims=False)


def spread(parts, axis):
    return [parts[0]] + [shift(parts[k], axis, k) for k in range(1, len(parts))]


def give_back(parts, axis):
    return [parts[0]] + [shift(parts[k], axis, -k) for k in range(1, len(parts))]


def scatter_sum(value, axis, dim, wire=bf16):
    size = lax.axis_size(axis)
    index = lax.axis_index(axis)
    total = pick(value, index, dim)
    for k in range(1, size):
        part = pick(value, lax.rem(index + k, size), dim).astype(wire)
        total = total + shift(part, axis, k).astype(f32)
    return total


def sum_everywhere(value, axes):
    for axis in axes:
        size = lax.axis_size(axis)
        step = 1
        while step < size:
            value = value + lax.ppermute(value, axis, [(i, i ^ step) for i in range(size)])
            step *= 2
    return value


def scatter_rows(value, wire=bf16):
    ga, gb, ctx, dp = (lax.axis_size(a) for a in ("ga", "gb", "context", "dp"))
    rows, cols = value.shape
    own = rows // (ga * gb * ctx * dp)
    value = value.reshape(ga, gb, ctx * dp * own, cols)
    value = scatter_sum(value, "gb", 1, wire)
    value = scatter_sum(value, "ga", 0, wire)
    value = value.reshape(ctx, dp, own, cols)
    value = scatter_sum(value, "dp", 1, wire)
    return scatter_sum(value, "context", 0, wire)


def split_halves(value):
    high = value.astype(bf16)
    return high, (value - high.astype(f32)).astype(bf16)


def gelu_parts(values):
    c = 0.7978845608028654
    square = values * values
    bent = jnp.tanh(c * values * (1.0 + 0.044715 * square))
    act = 0.5 * values * (1.0 + bent)
    slope = 0.5 * (1.0 + bent) + 0.5 * values * (1.0 - bent * bent) * c * (
        1.0 + 3 * 0.044715 * square
    )
    return act, slope


def local(
    tokens,
    cotangent,
    query_key_value_weight,
    output_weight,
    gain_one,
    gain_two,
    router_weight,
    w_in,
    w_down,
    position_bias,
    bucket,
    route,
    slot,
    dropped,
):
    seq_count, tok_count = tokens.shape[:2]
    row_count = seq_count * tok_count
    ga, gb, ctx = (lax.axis_size(a) for a in ("ga", "gb", "context"))
    experts = ga * gb
    seq_len = tok_count * experts * ctx
    chunk = ctx * tok_count
    capacity = (5 * row_count + 4 * experts - 1) // (4 * experts)
    expert_axis = ("ga", "gb")
    group_axis = ("ga", "context")
    ga_index, gb_index = lax.axis_index("ga"), lax.axis_index("gb")
    expert_index = lax.axis_index(expert_axis)
    head_group = lax.rem(lax.axis_index(group_axis), HEAD_GROUPS)

    inputs = tokens.reshape(row_count, D).astype(f32)
    scale_one = lax.rsqrt(jnp.mean(inputs * inputs, axis=-1, keepdims=True) + norm_epsilon)
    normed_low = (inputs * scale_one * gain_one).astype(bf16)
    projected = lax.dot_general(
        query_key_value_weight,
        normed_low,
        (((0,), (1,)), ((), ())),
        preferred_element_type=f32,
    ).astype(bf16)
    projected = projected.reshape(3, HEAD_GROUPS, GROUP_HEADS, HEAD_DIM, seq_count, tok_count)
    projected = jnp.transpose(projected, (4, 1, 2, 0, 3, 5)).reshape(
        GROUPS, GROUP_HEADS * 3 * HEAD_DIM, tok_count
    )
    gathered = lax.all_to_all(projected, group_axis, 0, 0, tiled=True)
    gathered = jnp.transpose(
        gathered.reshape(GROUPS, GROUP_HEADS, 3 * HEAD_DIM, tok_count), (1, 2, 0, 3)
    ).reshape(GROUP_HEADS, 3 * HEAD_DIM, GROUPS * tok_count)
    query = gathered[:, :HEAD_DIM]
    own_keys = gathered[:, HEAD_DIM:]
    key_value = jnp.concatenate(
        [own_keys] + [shift(own_keys, "gb", k) for k in range(1, gb)], axis=2
    )
    in_chunk = jnp.arange(ga, dtype=jnp.int32)[None, :] * gb
    peers = lax.rem(gb_index - jnp.arange(gb, dtype=jnp.int32) + gb, gb)[:, None]
    key_starts = ((in_chunk + peers) * chunk).reshape(-1).astype(jnp.int32)
    query_starts = key_starts[:ga]

    onehot = (
        jnp.arange(position_bias.shape[0], dtype=jnp.int32)[:, None]
        == jnp.pad(bucket[::-1], (0, 1), constant_values=-1)[None, :]
    ).astype(f32)
    bias_heads = lax.dynamic_slice_in_dim(position_bias.T, head_group * GROUP_HEADS, GROUP_HEADS, 0)
    table = jnp.dot(bias_heads, onehot, precision=precise_mode, preferred_element_type=f32)
    table = table[:, None, :]

    route_flat = route.reshape(-1)
    relative = lax.rem(route_flat - expert_index + experts, experts)
    position = relative * capacity + slot.reshape(-1)
    assign = (
        (jnp.arange(experts * capacity, dtype=jnp.int32)[:, None] == position[None, :])
        & (dropped.reshape(-1) == 0)[None, :]
    ).astype(bf16)
    grad_low = cotangent.reshape(row_count, D)
    grad_low, key_value = lax.optimization_barrier((grad_low, key_value))
    grad_buffer = matmul(assign, grad_low).astype(bf16).reshape(experts, capacity, D)
    grad_rows = jnp.concatenate(
        spread([grad_buffer[k] for k in range(experts)], expert_axis), axis=0
    )
    grad_blocks = spread([grad_rows] * ctx, "context")

    attended, lse = attention_forward(chunk, query_starts, key_starts, table, query, key_value)
    attended_parts = jnp.transpose(
        attended.astype(bf16).reshape(GROUP_HEADS * HEAD_DIM, GROUPS, tok_count), (1, 0, 2)
    )
    attended_parts = lax.all_to_all(attended_parts, group_axis, 0, 0, tiled=True)
    attended_low = jnp.transpose(
        attended_parts.reshape(seq_count, D, tok_count), (1, 0, 2)
    ).reshape(D, row_count)
    middle = inputs + contract_rows(attended_low, output_weight)
    scale_two = lax.rsqrt(jnp.mean(middle * middle, axis=-1, keepdims=True) + norm_epsilon)
    normalized_second = middle * scale_two * gain_two
    router_logits = jnp.dot(
        normalized_second, router_weight, precision=precise_mode, preferred_element_type=f32
    )
    router = jax.nn.softmax(router_logits, axis=-1)
    chosen = (route_flat[:, None] == jnp.arange(experts, dtype=jnp.int32)[None, :]).astype(f32)
    gate = jnp.sum(router * chosen, axis=-1, keepdims=True)

    gate_high, gate_low = split_halves(gate)
    payload = jnp.concatenate(
        [
            normalized_second.astype(bf16),
            gate_high,
            gate_low,
            jnp.zeros((row_count, 126), bf16),
        ],
        axis=1,
    )
    buffer = matmul(assign, payload).astype(bf16).reshape(experts, capacity, D + 128)
    received = jnp.concatenate(
        spread([buffer[k] for k in range(experts)], expert_axis), axis=0
    )
    row_blocks = spread([received[:, :D]] * ctx, "context")
    gate_blocks = spread([received[:, D:]] * ctx, "context")

    local_in = w_in[0]
    local_down = w_down[0]
    ones = jnp.ones((8, local_in.shape[1]), bf16)
    hidden_blocks, slope_blocks, back_parts, out_parts, gate_parts = [], [], [], [], []
    for k in range(ctx):
        act, slope = gelu_parts(matmul(row_blocks[k], local_in))
        hidden = act.astype(bf16)
        grad_hidden = matmul(grad_blocks[k], local_down)
        grad_pre = grad_hidden * slope
        hidden_blocks.append(hidden)
        slope_blocks.append(grad_pre)
        back_parts.append(contract_cols(grad_pre.astype(bf16), local_in).astype(bf16))
        gate_parts.append(contract_cols(ones, (grad_hidden * hidden.astype(f32)).astype(bf16)))
        out_parts.append(contract_cols(hidden, local_down).astype(bf16))

    def add_up(parts):
        total = parts[0].astype(f32)
        for part in parts[1:]:
            total = total + part.astype(f32)
        return total

    back_sum = add_up(give_back(back_parts, "context")).astype(bf16)
    gate_sum = add_up(give_back(gate_parts, "context"))
    back_rows = jnp.concatenate(
        give_back(
            [back_sum[k * capacity : (k + 1) * capacity] for k in range(experts)], expert_axis
        ),
        axis=0,
    )
    gate_row = jnp.concatenate(
        give_back(
            [gate_sum[:, k * capacity : (k + 1) * capacity] for k in range(experts)], expert_axis
        ),
        axis=1,
    )
    grad_sent = contract_rows(assign, back_rows) * gate
    grad_gate = lax.dot_general(
        assign.astype(f32),
        gate_row,
        (((0,), (1,)), ((), ())),
        precision=precise_mode,
        preferred_element_type=f32,
    )[:, :1]

    grad_out = cotangent.reshape(row_count, D).astype(f32)
    grad_logits = grad_gate * gate * (chosen - router)
    grad_normed_two = grad_sent + lax.dot_general(
        grad_logits,
        router_weight,
        (((1,), (1,)), ((), ())),
        precision=precise_mode,
        preferred_element_type=f32,
    )
    scaled_two = gain_two * grad_normed_two
    cube_two = scale_two * scale_two * scale_two
    grad_middle = (
        grad_out
        + scale_two * scaled_two
        - middle * cube_two * jnp.mean(scaled_two * middle, axis=-1, keepdims=True)
    )
    grad_branch = grad_middle.astype(bf16)

    grad_heads = contract_cols(output_weight, grad_branch).astype(bf16)
    grad_heads = jnp.transpose(
        grad_heads.reshape(HEAD_GROUPS, GROUP_HEADS * HEAD_DIM, seq_count, tok_count), (2, 0, 1, 3)
    ).reshape(GROUPS, GROUP_HEADS * HEAD_DIM, tok_count)
    grad_heads = lax.all_to_all(grad_heads, group_axis, 0, 0, tiled=True)
    grad_heads = jnp.transpose(
        grad_heads.reshape(GROUPS, GROUP_HEADS, HEAD_DIM, tok_count), (1, 2, 0, 3)
    ).reshape(GROUP_HEADS, HEAD_DIM, GROUPS * tok_count)
    grad_query, grad_kv, grad_table = attention_backward(
        chunk, query_starts, key_starts, table, query, key_value, attended, lse, grad_heads
    )
    grad_kv = grad_kv.reshape(GROUP_HEADS, 2 * HEAD_DIM, gb, GROUPS * tok_count)
    grad_kv = add_up(give_back([grad_kv[:, :, k] for k in range(gb)], "gb")).astype(bf16)
    grad_projected = jnp.concatenate([grad_query, grad_kv], axis=1)
    grad_projected = jnp.transpose(
        grad_projected.reshape(GROUP_HEADS * 3 * HEAD_DIM, GROUPS, tok_count), (1, 0, 2)
    )
    grad_projected = lax.all_to_all(grad_projected, group_axis, 0, 0, tiled=True)
    grad_projected = jnp.transpose(
        grad_projected.reshape(
            seq_count, HEAD_GROUPS, GROUP_HEADS, 3, HEAD_DIM, tok_count
        ),
        (3, 1, 2, 4, 0, 5),
    ).reshape(3 * D, row_count)
    qkv_grad = lax.dot_general(
        normed_low, grad_projected, (((0,), (1,)), ((), ())), preferred_element_type=f32
    )
    grad_normed = lax.dot_general(
        grad_projected,
        query_key_value_weight,
        (((0,), (1,)), ((), ())),
        preferred_element_type=f32,
    )
    scaled_one = gain_one * grad_normed
    cube_one = scale_one * scale_one * scale_one
    grad_inputs = (
        grad_middle
        + scale_one * scaled_one
        - inputs * cube_one * jnp.mean(scaled_one * inputs, axis=-1, keepdims=True)
    )
    gain_one_grad = jnp.sum(grad_normed * inputs * scale_one, axis=0)

    result = add_up(give_back(out_parts, "context")).astype(bf16)
    returned_rows = jnp.concatenate(
        give_back(
            [result[k * capacity : (k + 1) * capacity] for k in range(experts)], expert_axis
        ),
        axis=0,
    )
    returned = contract_rows(assign, returned_rows)
    output = (middle + gate * returned).astype(bf16)

    all_rows = jnp.concatenate(row_blocks, axis=0)
    all_grads = jnp.concatenate(grad_blocks, axis=0)
    all_gates = jnp.concatenate(gate_blocks, axis=0)[:, :2].astype(f32)
    all_gates = all_gates[:, :1] + all_gates[:, 1:2]
    all_hidden = jnp.concatenate(hidden_blocks, axis=0)
    all_pre = (jnp.concatenate(slope_blocks, axis=0) * all_gates).astype(bf16)
    all_returned = (all_gates * all_grads.astype(f32)).astype(bf16)
    down_part = contract_rows(all_returned, all_hidden)
    in_part = contract_rows(all_rows, all_pre)
    dp_size = lax.axis_size("dp")
    in_grad = scatter_sum(in_part.reshape(D, dp_size, -1), "dp", 1)
    down_grad = scatter_sum(down_part.reshape(D, dp_size, -1), "dp", 1)

    out_grad = scatter_rows(matmul(attended_low, grad_branch))
    router_grad = lax.dot_general(
        normalized_second,
        grad_logits,
        (((0,), (0,)), ((), ())),
        precision=precise_mode,
        preferred_element_type=f32,
    )
    gain_two_grad = jnp.sum(grad_normed_two * middle * scale_two, axis=0)
    small = scatter_rows(
        jnp.concatenate([router_grad, gain_two_grad[:, None]], axis=1), f32
    )
    qkv_total = scatter_rows(qkv_grad)
    gain_one_total = scatter_rows(gain_one_grad[:, None], f32)
    span = bucket.shape[0]
    grad_table = jnp.pad(grad_table, ((0, 0), (0, 0), (0, 8)))
    by_offset = grad_table[:, 0, 1 : 1 + span]
    for r in range(1, 8):
        by_offset = by_offset + grad_table[:, r, r + 1 : r + 1 + span]
    bias_part = lax.dot_general(
        by_offset,
        onehot[:, :span],
        (((1,), (1,)), ((), ())),
        precision=precise_mode,
        preferred_element_type=f32,
    )
    bias_grad = lax.dynamic_update_slice_in_dim(
        jnp.zeros((HEADS, bias_part.shape[1]), f32), bias_part, head_group * GROUP_HEADS, 0
    )
    bias_grad = sum_everywhere(bias_grad, ("gb", "ga", "dp", "context")).T
    return (
        output.reshape(seq_count, tok_count, D),
        grad_inputs.astype(bf16).reshape(seq_count, tok_count, D),
        qkv_total,
        out_grad,
        gain_one_total[:, 0],
        small[:, -1],
        small[:, :-1],
        in_grad[None],
        down_grad[None],
        bias_grad,
    )


def solution(mesh):
    ctx = mesh.shape["context"]
    ga = max(GROUPS // ctx, 1)
    gb = mesh.shape["expert"] // ga
    fine = Mesh(
        mesh.devices.reshape(ga, gb, ctx, mesh.shape["dp"]), ("ga", "gb", "context", "dp")
    )
    expert = ("ga", "gb")
    blocks = ("ga", "gb", "context")
    everywhere = ("ga", "gb", "context", "dp")
    return jax.shard_map(
        local,
        mesh=fine,
        in_specs=(
            P("dp", blocks, None),
            P("dp", blocks, None),
            P(),
            P(),
            P(),
            P(),
            P(),
            P(expert, None, "context"),
            P(expert, None, "context"),
            P(),
            P(),
            P("dp", blocks),
            P("dp", blocks),
            P("dp", blocks),
        ),
        out_specs=(
            P("dp", blocks, None),
            P("dp", blocks, None),
            P(everywhere, None),
            P(everywhere, None),
            P(everywhere),
            P(everywhere),
            P(everywhere, None),
            P(expert, None, ("context", "dp")),
            P(expert, None, ("context", "dp")),
            P(),
        ),
        check_vma=False,
    )
```

time: 1040 us -> 580 us (0.56)
  waiting for transfers between devices: 471 us -> 198 us
  local copies, waits for them, and re-layouts: 306 us -> 126 us
  starting transfers between devices: 9.33 us -> 103 us
  matrix products: 131 us -> 57.3 us
  blocking collectives: 63.7 us -> 0 us
  Pallas kernels: 0 us -> 47 us
  between operations: 14.9 us -> 2.17 us
    reduce_scatter x6 -> x0, waiting for transfers between devices: 336 us -> none  [the longest x1 115 us: local(): lax.psum_scatter(qkv_grad, ('expert', 'context', 'dp'), scatter_dimension...]
    ppermute x0 -> x66, waiting for transfers between devices: none -> 166 us  [the longest x61 160 us: shift(): lax.ppermute(value, axis, [(i, (i + step) % size) for i in range(size)])]
    all_gather x4 -> x0, waiting for transfers between devices: 92.2 us -> none  [the longest x2 63.7 us: context_rows(): return lax.all_gather(rows_flat, 'context', axis=0, tiled=True)]
    ppermute x0 -> x66, starting transfers between devices: none -> 83.1 us  [the longest x61 81 us: shift(): lax.ppermute(value, axis, [(i, (i + step) % size) for i in range(size)])]
    dot_general x36 -> x17, matrix products: 88 us -> 26.1 us  [the longest x11 16.6 us: matmul(): return jnp.dot(left, right, preferred_element_type=f32)]
    dynamic_update_slice x20 -> x1, local copies, waits for them, and re-layouts: 58.8 us -> 0.06 us  [local(): lax.dynamic_update_slice_in_dim(jnp.zeros((HEADS, bias_part.shape[1]), f3...]
    pallas_call x0 -> x2, Pallas kernels: none -> 47 us  [the longest x1 29.7 us: attention_backward(): pl.pallas_call(functools.partial(backward_kernel, chunk), grid=(GROUP_HEA...]
    unnamed x1 -> x0, blocking collectives: 40.5 us -> none
  transfers between devices with their start and end apart: 14 -> 70, of which waited for: 11 -> 25; matrix products, arithmetic and copies ran while one was open for 23% -> 28% of each run, Pallas kernels for 0% -> 8%
where the time goes in v1:
time: 580 us; the launch traced here: 569 us
  waiting for transfers between devices  198 us (34%)
  local copies, waits for them, and re-layouts  126 us (22%)
  starting transfers between devices  103 us (18%)
  matrix products  57.3 us (10%)
  Pallas kernels  47 us (8%)
  other arithmetic  35.8 us (6%)
    ppermute x61, waiting for transfers between devices, shift(): lax.ppermute(value, axis, [(i, (i + step) % size) for i in range(size)])  160 us
    ppermute x61, starting transfers between devices, shift(): lax.ppermute(value, axis, [(i, (i + step) % size) for i in range(size)])  81 us
    unnamed x171, local copies, waits for them, and re-layouts  39 us
    pallas_call x1, Pallas kernels, attention_backward(): pl.pallas_call(functools.partial(backward_kernel, chunk), grid=(GROUP_HEA...  29.7 us
    all_to_all x1, waiting for transfers between devices, local(): gathered = lax.all_to_all(projected, group_axis, 0, 0, tiled=True)  18.5 us
    pallas_call x1, Pallas kernels, attention_forward(): pl.pallas_call(functools.partial(forward_kernel, chunk), grid=(GROUP_HEAD...  17.3 us
    dot_general x11, matrix products, matmul(): return jnp.dot(left, right, preferred_element_type=f32)  16.6 us
    dot_general x13, matrix products, contract_cols(): lax.dot_general(left, right, (((1,), (1,)), ((), ())), preferred_element_...  14.9 us
  transfers between devices with their start and end apart: 70, of which 25 were waited for; matrix products, arithmetic and copies ran while one was open for 28% of the time, Pallas kernels for 8%

profile of v1, /device:TPU:0, one launch (start us, length us, event | category | flops | bytes accessed | tf_op | source)
XLA Modules:
  0.0 569.0 jit_solution(7389526650907443829)
XLA Ops:
  4.5 2.1 fusion.1
  6.6 2.4 copy.101
  9.0 3.5 reshape.274
  12.5 2.6 copy.102
  15.1 7.4 %all-to-all-start = ((bf16[8,576,128]{2,1,0:T(8,128)(2,1)}), bf16[8,576,128]{2,1,0:T(8,128)(2,1)}, u32[]{:S(2)}, u32[]{:S(2)}) async-start(bf16[8,576,128]{2,1,0:T(8,128)(2,1)} %bitcast.325), calls=%async_computation | async-start | bytes 2359296 | tf_op jit(solution)/shard_map/all_to_all | solution.py:344
  33.5 18.5 %all-to-all-done = bf16[8,576,128]{2,1,0:T(8,128)(2,1)} async-done(((bf16[8,576,128]{2,1,0:T(8,128)(2,1)}), bf16[8,576,128]{2,1,0:T(8,128)(2,1)}, u32[]{:S(2)}, u32[]{:S(2)}) %all-to-all-start) | async-done | bytes 1179680 | tf_op jit(solution)/shard_map/all_to_all | solution.py:344
  52.0 3.0 copy.174
  55.1 3.0 reshape.277
  65.6 17.3 %attention_forward.1 = (f32[3,64,1024]{2,1,0:T(8,128)S(1)}, f32[3,1,1024]{2,1,0:T(1,128)S(1)}) custom-call(s32[2]{0:T(128)S(1)} %slice_bitcast_fusion.1.qs_ref, s32[4]{0:T(128)S(1)} %mul.406.ks_ref, f32[3,1,4096]{2,1,0:T(1,128)S(1)} %copy-done.12, bf16[3,64,1024]{2,1,0:T(8,128)(2,1)S(1)} %slice.183.q_ref, bf16[3,128,2048]{2,1,0:T(8,128)(2,1)S(1)} %pad_maximum_fusion.kv_ref), custom_call_target="tpu_custom_call" | custom-call | flops 6442450944 | bytes 4718592 | tf_op jit(solution)/shard_map/attention_forward/pallas_call | solution.py:164
  85.3 4.1 all-to-all-start.1
  90.5 2.9 collective-permute-start.18
  94.9 2.4 collective-permute-start.20
  100.3 3.1 fusion.42
  105.0 17.3 %collective-permute-done.16 = bf16[320,768]{1,0:T(8,128)(2,1)S(1)} collective-permute-done((bf16[320,768]{1,0:T(8,128)(2,1)S(1)}, bf16[320,768]{1,0:T(8,128)(2,1)S(1)}, u32[]{:S(2)}, u32[]{:S(2)}) %collective-permute-start.16) | collective-permute-done | bytes 491552 | tf_op jit(solution)/shard_map/ppermute | solution.py:239
  124.6 9.3 %collective-permute-done.18 = bf16[320,768]{1,0:T(8,128)(2,1)S(1)} collective-permute-done((bf16[320,768]{1,0:T(8,128)(2,1)S(1)}, bf16[320,768]{1,0:T(8,128)(2,1)S(1)}, u32[]{:S(2)}, u32[]{:S(2)}) %collective-permute-start.18) | collective-permute-done | bytes 491552 | tf_op jit(solution)/shard_map/ppermute | solution.py:239
  140.5 2.1 multiply_reduce_fusion.2
  155.2 2.1 copy.117
  162.8 12.0 %collective-permute-start.57 = (bf16[320,128]{1,0:T(8,128)(2,1)S(1)}, bf16[320,128]{1,0:T(8,128)(2,1)S(1)}, u32[]{:S(2)}, u32[]{:S(2)}) collective-permute-start(bf16[320,128]{1,0:T(8,128)(2,1)S(1)} %pad_maximum_fusion.7), channel_id=1, source_target_pairs={{0,4},{2,6},{4,0},{6,2},{1,5},{3,7},{5,1},{7,3},{8,12},{10,14},{12... | collective-permute-start | bytes 245768 | tf_op jit(solution)/shard_map/ppermute | solution.py:239
  183.9 9.1 %collective-permute-done.8 = bf16[320,768]{1,0:T(8,128)(2,1)S(1)} collective-permute-done((bf16[320,768]{1,0:T(8,128)(2,1)S(1)}, bf16[320,768]{1,0:T(8,128)(2,1)S(1)}, u32[]{:S(2)}, u32[]{:S(2)}) %collective-permute-start.8) | collective-permute-done | bytes 491552 | tf_op jit(solution)/shard_map/ppermute | solution.py:239
  195.6 18.6 %collective-permute-done.4 = bf16[320,768]{1,0:T(8,128)(2,1)S(1)} collective-permute-done((bf16[320,768]{1,0:T(8,128)(2,1)S(1)}, bf16[320,768]{1,0:T(8,128)(2,1)S(1)}, u32[]{:S(2)}, u32[]{:S(2)}) %collective-permute-start.4) | collective-permute-done | bytes 491552 | tf_op jit(solution)/shard_map/ppermute | solution.py:239
  216.9 8.3 %collective-permute-done.6 = bf16[320,768]{1,0:T(8,128)(2,1)S(1)} collective-permute-done((bf16[320,768]{1,0:T(8,128)(2,1)S(1)}, bf16[320,768]{1,0:T(8,128)(2,1)S(1)}, u32[]{:S(2)}, u32[]{:S(2)}) %collective-permute-start.6) | collective-permute-done | bytes 491552 | tf_op jit(solution)/shard_map/ppermute | solution.py:239
  230.9 2.3 collective-permute-start.25
  237.8 3.5 fusion.2
  242.4 2.0 fusion.3
  251.7 2.7 copy.123
  254.4 2.1 copy.141
  256.5 2.7 copy.121
  259.2 2.1 copy.140
  261.3 2.2 collective-permute-start.5
  267.0 2.4 fusion.73
  273.7 3.0 collective-permute-start.19
  276.7 9.8 %collective-permute-done.5 = bf16[320,768]{1,0:T(8,128)(2,1)} collective-permute-done((bf16[320,768]{1,0:T(8,128)(2,1)}, bf16[320,768]{1,0:T(8,128)(2,1)}, u32[]{:S(2)}, u32[]{:S(2)}) %collective-permute-start.5) | collective-permute-done | bytes 491552 | tf_op jit(solution)/shard_map/ppermute | solution.py:239
  288.0 40.6 %collective-permute-done.7 = bf16[320,768]{1,0:T(8,128)(2,1)} collective-permute-done((bf16[320,768]{1,0:T(8,128)(2,1)}, bf16[320,768]{1,0:T(8,128)(2,1)}, u32[]{:S(2)}, u32[]{:S(2)}) %collective-permute-start.7) | collective-permute-done | bytes 491552 | tf_op jit(solution)/shard_map/ppermute | solution.py:239
  330.1 2.4 add_convert_fusion.1
  333.4 5.5 collective-permute-done.19
  358.5 4.1 all-to-all-start.2
  362.6 2.5 fusion.32
  368.5 3.1 fusion.111
  371.6 4.7 all-to-all-done.2
  384.9 29.7 %attention_backward.1 = (bf16[3,64,1024]{2,1,0:T(8,128)(2,1)S(1)}, bf16[3,128,2048]{2,1,0:T(8,128)(2,1)S(1)}, f32[3,8,4096]{2,1,0:T(8,128)S(1)}) custom-call(s32[2]{0:T(128)S(1)} %slice_bitcast_fusion.1.qs_ref, s32[4]{0:T(128)S(1)} %mul.406.ks_ref, f32[3,1,4096]{2,1,0:T(1,128)S(1)} %copy-done.13, bf16[3,64,1024]{2,1,0:T(8,128)(2,1)S(1)} %copy-done.10, ...), custom_call_target="tpu_custom_call" | custom-call | flops 16106127360 | bytes 9437184 | tf_op jit(solution)/shard_map/attention_backward/pallas_call | solution.py:198
  417.2 3.8 reshape.288
  421.0 5.6 fusion.206
  429.1 2.2 fusion.76
  435.9 2.1 fusion.22
  439.6 4.3 all-to-all-start.3
  444.0 2.6 fusion.27
  451.6 2.4 collective-permute-start.54
  457.6 2.6 bitcast_add_fusion.4
  464.8 9.5 %all-to-all-done.3 = bf16[8,576,128]{2,1,0:T(8,128)(2,1)} async-done(((bf16[8,576,128]{2,1,0:T(8,128)(2,1)}), bf16[8,576,128]{2,1,0:T(8,128)(2,1)}, u32[]{:S(2)}, u32[]{:S(2)}) %all-to-all-start.3) | async-done | bytes 1179680 | tf_op jit(solution)/shard_map/all_to_all | solution.py:495
  474.4 3.5 copy.114
  477.9 3.9 reshape.304
  481.8 2.5 fusion.34
  484.3 2.9 copy-done.16
  491.4 2.6 collective-permute-done.64
  495.6 2.9 collective-permute-done.65
  501.8 3.7 collective-permute-start.43
  506.6 2.7 fusion.71
  509.5 2.8 bitcast_add_fusion
  519.4 18.1 %collective-permute-done.45 = f32[192,1]{0,1:T(1,128)S(1)} collective-permute-done((f32[192,1]{0,1:T(1,128)S(1)}, f32[192,1]{0,1:T(1,128)S(1)}, u32[]{:S(2)}, u32[]{:S(2)}) %collective-permute-start.45) | collective-permute-done | bytes 800 | tf_op jit(solution)/shard_map/ppermute | solution.py:239
  537.6 2.0 bitcast_add_fusion.1
  542.9 8.7 %collective-permute-done.46 = f32[4,24,1]{1,0,2:T(4,128)S(1)} collective-permute-done((f32[4,24,1]{1,0,2:T(4,128)S(1)}, f32[4,24,1]{1,0,2:T(4,128)S(1)}, u32[]{:S(2)}, u32[]{:S(2)}) %collective-permute-start.46) | collective-permute-done | bytes 416 | tf_op jit(solution)/shard_map/ppermute | solution.py:239
  551.7 3.8 collective-permute-start.49
  556.3 3.3 collective-permute-start.37
  563.2 4.6 collective-permute-done.36
  (408 shorter events, 185.2 us)
Async XLA Ops:
  15.1 36.9 %all-to-all-start = ((bf16[8,576,128]{2,1,0:T(8,128)(2,1)}), bf16[8,576,128]{2,1,0:T(8,128)(2,1)}, u32[]{:S(2)}, u32[]{:S(2)}) async-start(bf16[8,576,128]{2,1,0:T(8,128)(2,1)} %bitcast.325), calls=%async_computation | async-start | bytes 2359296 | tf_op jit(solution)/shard_map/all_to_all | solution.py:344
  63.5 25.9 %collective-permute-start.15 = (bf16[80,768]{1,0:T(8,128)(2,1)}, bf16[80,768]{1,0:T(8,128)(2,1)}, u32[]{:S(2)}, u32[]{:S(2)}) collective-permute-start(bf16[80,768]{1,0:T(8,128)(2,1)} %get-tuple-element.48), channel_id=1, source_target_pairs={{0,24},{8,0},{16,8},{24,16},{1,25},{9,1},{17,9},{25,17},{2,26},{10... | collective-permute-start | bytes 368648 | tf_op jit(solution)/shard_map/ppermute | solution.py:239
  64.1 25.3 %collective-permute-start.14 = (bf16[80,768]{1,0:T(8,128)(2,1)}, bf16[80,768]{1,0:T(8,128)(2,1)}, u32[]{:S(2)}, u32[]{:S(2)}) collective-permute-start(bf16[80,768]{1,0:T(8,128)(2,1)} %get-tuple-element.49), channel_id=1, source_target_pairs={{0,16},{8,24},{16,0},{24,8},{1,17},{9,25},{17,1},{25,9},{2,18},{10... | collective-permute-start | bytes 368648 | tf_op jit(solution)/shard_map/ppermute | solution.py:239
  65.6 23.8 %collective-permute-start.13 = (bf16[80,768]{1,0:T(8,128)(2,1)}, bf16[80,768]{1,0:T(8,128)(2,1)}, u32[]{:S(2)}, u32[]{:S(2)}) collective-permute-start(bf16[80,768]{1,0:T(8,128)(2,1)} %get-tuple-element.50), channel_id=1, source_target_pairs={{0,8},{8,16},{16,24},{24,0},{1,9},{9,17},{17,25},{25,1},{2,10},{10... | collective-permute-start | bytes 368648 | tf_op jit(solution)/shard_map/ppermute | solution.py:239
  85.3 53.3 %all-to-all-start.1 = ((bf16[8,192,128]{2,1,0:T(8,128)(2,1)}), bf16[8,192,128]{2,1,0:T(8,128)(2,1)}, u32[]{:S(2)}, u32[]{:S(2)}) async-start(bf16[8,192,128]{2,1,0:T(8,128)(2,1)} %bitcast.336), calls=%async_computation.1 | async-start | bytes 786432 | tf_op jit(solution)/shard_map/all_to_all | solution.py:385
  90.5 43.5 %collective-permute-start.18 = (bf16[320,768]{1,0:T(8,128)(2,1)S(1)}, bf16[320,768]{1,0:T(8,128)(2,1)S(1)}, u32[]{:S(2)}, u32[]{:S(2)}) collective-permute-start(bf16[320,768]{1,0:T(8,128)(2,1)S(1)} %pad_maximum_fusion.3), channel_id=1, source_target_pairs={{0,4},{2,6},{4,0},{6,2},{1,5},{3,7},{5,1},{7,3},{8,12},{10,14},{12... | collective-permute-start | bytes 1474568 | tf_op jit(solution)/shard_map/ppermute | solution.py:239
  93.4 28.9 %collective-permute-start.16 = (bf16[320,768]{1,0:T(8,128)(2,1)S(1)}, bf16[320,768]{1,0:T(8,128)(2,1)S(1)}, u32[]{:S(2)}, u32[]{:S(2)}) collective-permute-start(bf16[320,768]{1,0:T(8,128)(2,1)S(1)} %pad_maximum_fusion.3), channel_id=1, source_target_pairs={{0,2},{2,4},{4,6},{6,0},{1,3},{3,5},{5,7},{7,1},{8,10},{10,12},{12... | collective-permute-start | bytes 1474568 | tf_op jit(solution)/shard_map/ppermute | solution.py:239
  94.9 41.4 %collective-permute-start.20 = (bf16[320,768]{1,0:T(8,128)(2,1)S(1)}, bf16[320,768]{1,0:T(8,128)(2,1)S(1)}, u32[]{:S(2)}, u32[]{:S(2)}) collective-permute-start(bf16[320,768]{1,0:T(8,128)(2,1)S(1)} %pad_maximum_fusion.3), channel_id=1, source_target_pairs={{0,6},{2,0},{4,2},{6,4},{1,7},{3,1},{5,3},{7,5},{8,14},{10,8},{12,... | collective-permute-start | bytes 1474568 | tf_op jit(solution)/shard_map/ppermute | solution.py:239
  151.4 8.0 %collective-permute-start.3 = (bf16[80,896]{1,0:T(8,128)(2,1)}, bf16[80,896]{1,0:T(8,128)(2,1)}, u32[]{:S(2)}, u32[]{:S(2)}) collective-permute-start(bf16[80,896]{1,0:T(8,128)(2,1)} %get-tuple-element.44), channel_id=1, source_target_pairs={{0,24},{8,0},{16,8},{24,16},{1,25},{9,1},{17,9},{25,17},{2,26},{10... | collective-permute-start | bytes 430088 | tf_op jit(solution)/shard_map/ppermute | solution.py:239
  152.0 8.8 %collective-permute-start.2 = (bf16[80,896]{1,0:T(8,128)(2,1)}, bf16[80,896]{1,0:T(8,128)(2,1)}, u32[]{:S(2)}, u32[]{:S(2)}) collective-permute-start(bf16[80,896]{1,0:T(8,128)(2,1)} %get-tuple-element.45), channel_id=1, source_target_pairs={{0,16},{8,24},{16,0},{24,8},{1,17},{9,25},{17,1},{25,9},{2,18},{10... | collective-permute-start | bytes 430088 | tf_op jit(solution)/shard_map/ppermute | solution.py:239
  152.9 8.0 %collective-permute-start.1 = (bf16[80,896]{1,0:T(8,128)(2,1)}, bf16[80,896]{1,0:T(8,128)(2,1)}, u32[]{:S(2)}, u32[]{:S(2)}) collective-permute-start(bf16[80,896]{1,0:T(8,128)(2,1)} %get-tuple-element.46), channel_id=1, source_target_pairs={{0,8},{8,16},{16,24},{24,0},{1,9},{9,17},{17,25},{25,1},{2,10},{10... | collective-permute-start | bytes 430088 | tf_op jit(solution)/shard_map/ppermute | solution.py:239
  161.7 19.3 %collective-permute-start.58 = (bf16[320,128]{1,0:T(8,128)(2,1)S(1)}, bf16[320,128]{1,0:T(8,128)(2,1)S(1)}, u32[]{:S(2)}, u32[]{:S(2)}) collective-permute-start(bf16[320,128]{1,0:T(8,128)(2,1)S(1)} %pad_maximum_fusion.7), channel_id=1, source_target_pairs={{0,6},{2,0},{4,2},{6,4},{1,7},{3,1},{5,3},{7,5},{8,14},{10,8},{12,... | collective-permute-start | bytes 245768 | tf_op jit(solution)/shard_map/ppermute | solution.py:239
  162.8 20.5 %collective-permute-start.57 = (bf16[320,128]{1,0:T(8,128)(2,1)S(1)}, bf16[320,128]{1,0:T(8,128)(2,1)S(1)}, u32[]{:S(2)}, u32[]{:S(2)}) collective-permute-start(bf16[320,128]{1,0:T(8,128)(2,1)S(1)} %pad_maximum_fusion.7), channel_id=1, source_target_pairs={{0,4},{2,6},{4,0},{6,2},{1,5},{3,7},{5,1},{7,3},{8,12},{10,14},{12... | collective-permute-start | bytes 245768 | tf_op jit(solution)/shard_map/ppermute | solution.py:239
  174.9 8.5 %collective-permute-start.56 = (bf16[320,128]{1,0:T(8,128)(2,1)S(1)}, bf16[320,128]{1,0:T(8,128)(2,1)S(1)}, u32[]{:S(2)}, u32[]{:S(2)}) collective-permute-start(bf16[320,128]{1,0:T(8,128)(2,1)S(1)} %pad_maximum_fusion.7), channel_id=1, source_target_pairs={{0,2},{2,4},{4,6},{6,0},{1,3},{3,5},{5,7},{7,1},{8,10},{10,12},{12... | collective-permute-start | bytes 245768 | tf_op jit(solution)/shard_map/ppermute | solution.py:239
  178.0 14.9 %collective-permute-start.8 = (bf16[320,768]{1,0:T(8,128)(2,1)S(1)}, bf16[320,768]{1,0:T(8,128)(2,1)S(1)}, u32[]{:S(2)}, u32[]{:S(2)}) collective-permute-start(bf16[320,768]{1,0:T(8,128)(2,1)S(1)} %slice.189), channel_id=1, source_target_pairs={{0,6},{2,0},{4,2},{6,4},{1,7},{3,1},{5,3},{7,5},{8,14},{10,8},{12,... | collective-permute-start | bytes 1474568 | tf_op jit(solution)/shard_map/ppermute | solution.py:239
  179.9 45.2 %collective-permute-start.6 = (bf16[320,768]{1,0:T(8,128)(2,1)S(1)}, bf16[320,768]{1,0:T(8,128)(2,1)S(1)}, u32[]{:S(2)}, u32[]{:S(2)}) collective-permute-start(bf16[320,768]{1,0:T(8,128)(2,1)S(1)} %slice.189), channel_id=1, source_target_pairs={{0,4},{2,6},{4,0},{6,2},{1,5},{3,7},{5,1},{7,3},{8,12},{10,14},{12... | collective-permute-start | bytes 1474568 | tf_op jit(solution)/shard_map/ppermute | solution.py:239
  181.0 33.2 %collective-permute-start.4 = (bf16[320,768]{1,0:T(8,128)(2,1)S(1)}, bf16[320,768]{1,0:T(8,128)(2,1)S(1)}, u32[]{:S(2)}, u32[]{:S(2)}) collective-permute-start(bf16[320,768]{1,0:T(8,128)(2,1)S(1)} %slice.189), channel_id=1, source_target_pairs={{0,2},{2,4},{4,6},{6,0},{1,3},{3,5},{5,7},{7,1},{8,10},{10,12},{12... | collective-permute-start | bytes 1474568 | tf_op jit(solution)/shard_map/ppermute | solution.py:239
  227.8 18.6 %collective-permute-start.27 = (f32[8,320]{1,0:T(8,128)S(1)}, f32[8,320]{1,0:T(8,128)S(1)}, u32[]{:S(2)}, u32[]{:S(2)}) collective-permute-start(f32[8,320]{1,0:T(8,128)S(1)} %fusion.81), channel_id=1, source_target_pairs={{0,2},{2,4},{4,6},{6,0},{1,3},{3,5},{5,7},{7,1},{8,10},{10,12},{12... | collective-permute-start | bytes 30728 | tf_op jit(solution)/shard_map/ppermute | solution.py:239
  230.9 15.5 %collective-permute-start.25 = (f32[8,320]{1,0:T(8,128)S(1)}, f32[8,320]{1,0:T(8,128)S(1)}, u32[]{:S(2)}, u32[]{:S(2)}) collective-permute-start(f32[8,320]{1,0:T(8,128)S(1)} %fusion.79), channel_id=1, source_target_pairs={{0,6},{2,0},{4,2},{6,4},{1,7},{3,1},{5,3},{7,5},{8,14},{10,8},{12,... | collective-permute-start | bytes 30728 | tf_op jit(solution)/shard_map/ppermute | solution.py:239
  236.0 10.4 %collective-permute-start.26 = (f32[8,320]{1,0:T(8,128)S(1)}, f32[8,320]{1,0:T(8,128)S(1)}, u32[]{:S(2)}, u32[]{:S(2)}) collective-permute-start(f32[8,320]{1,0:T(8,128)S(1)} %fusion.80), channel_id=1, source_target_pairs={{0,4},{2,6},{4,0},{6,2},{1,5},{3,7},{5,1},{7,3},{8,12},{10,14},{12... | collective-permute-start | bytes 30728 | tf_op jit(solution)/shard_map/ppermute | solution.py:239
  247.3 13.9 %collective-permute-start.30 = (f32[8,80]{1,0:T(8,128)}, f32[8,80]{1,0:T(8,128)}, u32[]{:S(2)}, u32[]{:S(2)}) collective-permute-start(f32[8,80]{1,0:T(8,128)} %get-tuple-element.66), channel_id=1, source_target_pairs={{0,8},{8,16},{16,24},{24,0},{1,9},{9,17},{17,25},{25,1},{2,10},{10... | collective-permute-start | bytes 7688 | tf_op jit(solution)/shard_map/ppermute | solution.py:239
  247.4 16.1 %collective-permute-start.29 = (f32[8,80]{1,0:T(8,128)}, f32[8,80]{1,0:T(8,128)}, u32[]{:S(2)}, u32[]{:S(2)}) collective-permute-start(f32[8,80]{1,0:T(8,128)} %get-tuple-element.67), channel_id=1, source_target_pairs={{0,16},{8,24},{16,0},{24,8},{1,17},{9,25},{17,1},{25,9},{2,18},{10... | collective-permute-start | bytes 7688 | tf_op jit(solution)/shard_map/ppermute | solution.py:239
  247.7 17.7 %collective-permute-start.28 = (f32[8,80]{1,0:T(8,128)}, f32[8,80]{1,0:T(8,128)}, u32[]{:S(2)}, u32[]{:S(2)}) collective-permute-start(f32[8,80]{1,0:T(8,128)} %get-tuple-element.68), channel_id=1, source_target_pairs={{0,24},{8,0},{16,8},{24,16},{1,25},{9,1},{17,9},{25,17},{2,26},{10... | collective-permute-start | bytes 7688 | tf_op jit(solution)/shard_map/ppermute | solution.py:239
  250.0 23.7 %collective-permute-start.9 = (bf16[320,768]{1,0:T(8,128)(2,1)}, bf16[320,768]{1,0:T(8,128)(2,1)}, u32[]{:S(2)}, u32[]{:S(2)}) collective-permute-start(bf16[320,768]{1,0:T(8,128)(2,1)} %convolution_convert_fusion.7), channel_id=1, source_target_pairs={{0,2},{2,4},{4,6},{6,0},{1,3},{3,5},{5,7},{7,1},{8,10},{10,12},{12... | collective-permute-start | bytes 1474568 | tf_op jit(solution)/shard_map/ppermute | solution.py:239
  250.1 83.3 %collective-permute-start.21 = (bf16[320,768]{1,0:T(8,128)(2,1)}, bf16[320,768]{1,0:T(8,128)(2,1)}, u32[]{:S(2)}, u32[]{:S(2)}) collective-permute-start(bf16[320,768]{1,0:T(8,128)(2,1)} %convolution_convert_fusion.3), channel_id=1, source_target_pairs={{0,2},{2,4},{4,6},{6,0},{1,3},{3,5},{5,7},{7,1},{8,10},{10,12},{12... | collective-permute-start | bytes 1474568 | tf_op jit(solution)/shard_map/ppermute | solution.py:239
  261.3 25.2 %collective-permute-start.5 = (bf16[320,768]{1,0:T(8,128)(2,1)}, bf16[320,768]{1,0:T(8,128)(2,1)}, u32[]{:S(2)}, u32[]{:S(2)}) collective-permute-start(bf16[320,768]{1,0:T(8,128)(2,1)} %convolution_convert_fusion.9), channel_id=1, source_target_pairs={{0,6},{2,0},{4,2},{6,4},{1,7},{3,1},{5,3},{7,5},{8,14},{10,8},{12,... | collective-permute-start | bytes 1474568 | tf_op jit(solution)/shard_map/ppermute | solution.py:239
  263.5 69.9 %collective-permute-start.17 = (bf16[320,768]{1,0:T(8,128)(2,1)}, bf16[320,768]{1,0:T(8,128)(2,1)}, u32[]{:S(2)}, u32[]{:S(2)}) collective-permute-start(bf16[320,768]{1,0:T(8,128)(2,1)} %convolution_convert_fusion.5), channel_id=1, source_target_pairs={{0,6},{2,0},{4,2},{6,4},{1,7},{3,1},{5,3},{7,5},{8,14},{10,8},{12,... | collective-permute-start | bytes 1474568 | tf_op jit(solution)/shard_map/ppermute | solution.py:239
  265.5 63.1 %collective-permute-start.7 = (bf16[320,768]{1,0:T(8,128)(2,1)}, bf16[320,768]{1,0:T(8,128)(2,1)}, u32[]{:S(2)}, u32[]{:S(2)}) collective-permute-start(bf16[320,768]{1,0:T(8,128)(2,1)} %convolution_convert_fusion.8), channel_id=1, source_target_pairs={{0,4},{2,6},{4,0},{6,2},{1,5},{3,7},{5,1},{7,3},{8,12},{10,14},{12... | collective-permute-start | bytes 1474568 | tf_op jit(solution)/shard_map/ppermute | solution.py:239
  273.7 65.2 %collective-permute-start.19 = (bf16[320,768]{1,0:T(8,128)(2,1)}, bf16[320,768]{1,0:T(8,128)(2,1)S(1)}, u32[]{:S(2)}, u32[]{:S(2)}) collective-permute-start(bf16[320,768]{1,0:T(8,128)(2,1)} %convolution_convert_fusion.4), channel_id=1, source_target_pairs={{0,4},{2,6},{4,0},{6,2},{1,5},{3,7},{5,1},{7,3},{8,12},{10,14},{12... | collective-permute-start | bytes 1474568 | tf_op jit(solution)/shard_map/ppermute | solution.py:239
  286.5 55.2 %collective-permute-start.59 = (bf16[768,384]{1,0:T(8,128)(2,1)}, bf16[768,384]{1,0:T(8,128)(2,1)S(1)}, u32[]{:S(2)}, u32[]{:S(2)}) collective-permute-start(bf16[768,384]{1,0:T(8,128)(2,1)} %bitcast.349), channel_id=1, source_target_pairs={{0,1},{1,0},{2,3},{3,2},{4,5},{5,4},{6,7},{7,6},{8,9},{9,8},{10,11... | collective-permute-start | bytes 1769480 | tf_op jit(solution)/shard_map/ppermute | solution.py:239
  328.6 33.9 %collective-permute-start.60 = (bf16[768,384]{1,0:T(8,128)(2,1)}, bf16[768,384]{1,0:T(8,128)(2,1)}, u32[]{:S(2)}, u32[]{:S(2)}) collective-permute-start(bf16[768,384]{1,0:T(8,128)(2,1)} %bitcast.348), channel_id=1, source_target_pairs={{0,1},{1,0},{2,3},{3,2},{4,5},{5,4},{6,7},{7,6},{8,9},{9,8},{10,11... | collective-permute-start | bytes 1769480 | tf_op jit(solution)/shard_map/ppermute | solution.py:239
  333.4 110.6 %collective-permute-start.12 = (bf16[80,768]{1,0:T(8,128)(2,1)}, bf16[80,768]{1,0:T(8,128)(2,1)}, u32[]{:S(2)}, u32[]{:S(2)}) collective-permute-start(bf16[80,768]{1,0:T(8,128)(2,1)} %get-tuple-element.57), channel_id=1, source_target_pairs={{0,8},{8,16},{16,24},{24,0},{1,9},{9,17},{17,25},{25,1},{2,10},{10... | collective-permute-start | bytes 368648 | tf_op jit(solution)/shard_map/ppermute | solution.py:239
  340.9 5.1 collective-permute-start.24
  341.0 6.2 %collective-permute-start.23 = (bf16[80,768]{1,0:T(8,128)(2,1)S(1)}, bf16[80,768]{1,0:T(8,128)(2,1)S(1)}, u32[]{:S(2)}, u32[]{:S(2)}) collective-permute-start(bf16[80,768]{1,0:T(8,128)(2,1)S(1)} %get-tuple-element.54), channel_id=1, source_target_pairs={{0,16},{8,24},{16,0},{24,8},{1,17},{9,25},{17,1},{25,9},{2,18},{10... | collective-permute-start | bytes 368648 | tf_op jit(solution)/shard_map/ppermute | solution.py:239
  341.7 7.2 %collective-permute-start.22 = (bf16[80,768]{1,0:T(8,128)(2,1)S(1)}, bf16[80,768]{1,0:T(8,128)(2,1)S(1)}, u32[]{:S(2)}, u32[]{:S(2)}) collective-permute-start(bf16[80,768]{1,0:T(8,128)(2,1)S(1)} %get-tuple-element.55), channel_id=1, source_target_pairs={{0,24},{8,0},{16,8},{24,16},{1,25},{9,1},{17,9},{25,17},{2,26},{10... | collective-permute-start | bytes 368648 | tf_op jit(solution)/shard_map/ppermute | solution.py:239
  345.9 98.0 %collective-permute-start.11 = (bf16[80,768]{1,0:T(8,128)(2,1)}, bf16[80,768]{1,0:T(8,128)(2,1)}, u32[]{:S(2)}, u32[]{:S(2)}) collective-permute-start(bf16[80,768]{1,0:T(8,128)(2,1)} %get-tuple-element.58), channel_id=1, source_target_pairs={{0,16},{8,24},{16,0},{24,8},{1,17},{9,25},{17,1},{25,9},{2,18},{10... | collective-permute-start | bytes 368648 | tf_op jit(solution)/shard_map/ppermute | solution.py:239
  347.2 96.8 %collective-permute-start.10 = (bf16[80,768]{1,0:T(8,128)(2,1)}, bf16[80,768]{1,0:T(8,128)(2,1)}, u32[]{:S(2)}, u32[]{:S(2)}) collective-permute-start(bf16[80,768]{1,0:T(8,128)(2,1)} %get-tuple-element.59), channel_id=1, source_target_pairs={{0,24},{8,0},{16,8},{24,16},{1,25},{9,1},{17,9},{25,17},{2,26},{10... | collective-permute-start | bytes 368648 | tf_op jit(solution)/shard_map/ppermute | solution.py:239
  358.5 17.8 %all-to-all-start.2 = ((bf16[8,192,128]{2,1,0:T(8,128)(2,1)}), bf16[8,192,128]{2,1,0:T(8,128)(2,1)}, u32[]{:S(2)}, u32[]{:S(2)}) async-start(bf16[8,192,128]{2,1,0:T(8,128)(2,1)} %bitcast.337), calls=%async_computation.2 | async-start | bytes 786432 | tf_op jit(solution)/shard_map/all_to_all | solution.py:482
  367.8 60.0 %collective-permute-start.50 = (f32[2,192,5]{1,0,2:T(2,128)}, f32[2,192,5]{1,0,2:T(2,128)}, u32[]{:S(2)}, u32[]{:S(2)}) collective-permute-start(f32[2,192,5]{1,0,2:T(2,128)} %fusion.160), channel_id=1, source_target_pairs={{0,8},{8,0},{1,9},{9,1},{2,10},{10,2},{3,11},{11,3},{4,12},{12,4},... | collective-permute-start | bytes 23048 | tf_op jit(solution)/shard_map/ppermute | solution.py:239
  427.8 6.6 %collective-permute-start.31 = (bf16[3,128,1024]{2,1,0:T(8,128)(2,1)}, bf16[3,128,1024]{2,1,0:T(8,128)(2,1)}, u32[]{:S(2)}, u32[]{:S(2)}) collective-permute-start(bf16[3,128,1024]{2,1,0:T(8,128)(2,1)} %bitcast.314), channel_id=1, source_target_pairs={{0,8},{8,0},{1,9},{9,1},{2,10},{10,2},{3,11},{11,3},{4,12},{12,4},... | collective-permute-start | bytes 2359304 | tf_op jit(solution)/shard_map/ppermute | solution.py:239
  432.2 25.4 %collective-permute-start.38 = (bf16[2,192,768]{2,1,0:T(8,128)(2,1)}, bf16[2,192,768]{2,1,0:T(8,128)(2,1)}, u32[]{:S(2)}, u32[]{:S(2)}) collective-permute-start(bf16[2,192,768]{2,1,0:T(8,128)(2,1)} %fusion.76), channel_id=1, source_target_pairs={{0,8},{8,0},{1,9},{9,1},{2,10},{10,2},{3,11},{11,3},{4,12},{12,4},... | collective-permute-start | bytes 1769480 | tf_op jit(solution)/shard_map/ppermute | solution.py:239
  434.4 12.2 %collective-permute-start.52 = (f32[4,24,5]{1,0,2:T(4,128)}, f32[4,24,5]{1,0,2:T(4,128)}, u32[]{:S(2)}, u32[]{:S(2)}) collective-permute-start(f32[4,24,5]{1,0,2:T(4,128)} %bitcast.72), channel_id=1, source_target_pairs={{0,1},{1,0},{2,3},{3,2},{4,5},{5,4},{6,7},{7,6},{8,9},{9,8},{10,11... | collective-permute-start | bytes 5768 | tf_op jit(solution)/shard_map/ppermute | solution.py:239
  439.6 34.7 %all-to-all-start.3 = ((bf16[8,576,128]{2,1,0:T(8,128)(2,1)}), bf16[8,576,128]{2,1,0:T(8,128)(2,1)}, u32[]{:S(2)}, u32[]{:S(2)}) async-start(bf16[8,576,128]{2,1,0:T(8,128)(2,1)} %bitcast.326), calls=%async_computation.3 | async-start | bytes 2359296 | tf_op jit(solution)/shard_map/all_to_all | solution.py:495
  449.7 39.0 %collective-permute-start.53 = (f32[24,5]{0,1:T(8,128)}, f32[24,5]{0,1:T(8,128)}, u32[]{:S(2)}, u32[]{:S(2)}) collective-permute-start(f32[24,5]{0,1:T(8,128)} %bitcast.320), channel_id=1, source_target_pairs={{0,2},{2,4},{4,6},{6,0},{1,3},{3,5},{5,7},{7,1},{8,10},{10,12},{12... | collective-permute-start | bytes 1448 | tf_op jit(solution)/shard_map/ppermute | solution.py:239
  451.6 37.2 %collective-permute-start.54 = (f32[24,5]{0,1:T(8,128)}, f32[24,5]{0,1:T(8,128)}, u32[]{:S(2)}, u32[]{:S(2)}) collective-permute-start(f32[24,5]{0,1:T(8,128)} %bitcast.319), channel_id=1, source_target_pairs={{0,4},{2,6},{4,0},{6,2},{1,5},{3,7},{5,1},{7,3},{8,12},{10,14},{12... | collective-permute-start | bytes 1448 | tf_op jit(solution)/shard_map/ppermute | solution.py:239
  453.9 34.9 %collective-permute-start.55 = (f32[24,5]{0,1:T(8,128)}, f32[24,5]{0,1:T(8,128)}, u32[]{:S(2)}, u32[]{:S(2)}) collective-permute-start(f32[24,5]{0,1:T(8,128)} %bitcast.318), channel_id=1, source_target_pairs={{0,6},{2,0},{4,2},{6,4},{1,7},{3,1},{5,3},{7,5},{8,14},{10,8},{12,... | collective-permute-start | bytes 1448 | tf_op jit(solution)/shard_map/ppermute | solution.py:239
  463.8 30.2 %collective-permute-start.39 = (bf16[192,768]{1,0:T(8,128)(2,1)}, bf16[192,768]{1,0:T(8,128)(2,1)}, u32[]{:S(2)}, u32[]{:S(2)}) collective-permute-start(bf16[192,768]{1,0:T(8,128)(2,1)} %fusion.124), channel_id=1, source_target_pairs={{0,16},{16,0},{1,17},{17,1},{2,18},{18,2},{3,19},{19,3},{4,20},{20... | collective-permute-start | bytes 884744 | tf_op jit(solution)/shard_map/ppermute | solution.py:239
  464.3 25.3 %collective-permute-start.63 = (f32[12,32]{1,0:T(8,128)S(1)}, f32[12,32]{1,0:T(8,128)}, u32[]{:S(2)}, u32[]{:S(2)}) collective-permute-start(f32[12,32]{1,0:T(8,128)S(1)} %add.507), channel_id=1, source_target_pairs={{0,1},{1,0},{2,3},{3,2},{4,5},{5,4},{6,7},{7,6},{8,9},{9,8},{10,11... | collective-permute-start | bytes 4616 | tf_op jit(solution)/shard_map/ppermute | solution.py:269
  488.7 20.8 %collective-permute-start.32 = (bf16[2,192,2304]{2,1,0:T(8,128)(2,1)}, bf16[2,192,2304]{2,1,0:T(8,128)(2,1)}, u32[]{:S(2)}, u32[]{:S(2)}) collective-permute-start(bf16[2,192,2304]{2,1,0:T(8,128)(2,1)} %fusion.21), channel_id=1, source_target_pairs={{0,8},{8,0},{1,9},{9,1},{2,10},{10,2},{3,11},{11,3},{4,12},{12,4},... | collective-permute-start | bytes 5308424 | tf_op jit(solution)/shard_map/ppermute | solution.py:239
  495.1 5.2 collective-permute-start.40
  501.7 14.0 %collective-permute-start.41 = (bf16[24,768]{1,0:T(8,128)(2,1)}, bf16[24,768]{1,0:T(8,128)(2,1)}, u32[]{:S(2)}, u32[]{:S(2)}) collective-permute-start(bf16[24,768]{1,0:T(8,128)(2,1)} %get-tuple-element.60), channel_id=1, source_target_pairs={{0,2},{2,4},{4,6},{6,0},{1,3},{3,5},{5,7},{7,1},{8,10},{10,12},{12... | collective-permute-start | bytes 110600 | tf_op jit(solution)/shard_map/ppermute | solution.py:239
  501.8 13.8 %collective-permute-start.43 = (bf16[24,768]{1,0:T(8,128)(2,1)}, bf16[24,768]{1,0:T(8,128)(2,1)}, u32[]{:S(2)}, u32[]{:S(2)}) collective-permute-start(bf16[24,768]{1,0:T(8,128)(2,1)} %get-tuple-element.61), channel_id=1, source_target_pairs={{0,6},{2,0},{4,2},{6,4},{1,7},{3,1},{5,3},{7,5},{8,14},{10,8},{12,... | collective-permute-start | bytes 110600 | tf_op jit(solution)/shard_map/ppermute | solution.py:239
  505.5 10.2 %collective-permute-start.42 = (bf16[24,768]{1,0:T(8,128)(2,1)}, bf16[24,768]{1,0:T(8,128)(2,1)}, u32[]{:S(2)}, u32[]{:S(2)}) collective-permute-start(bf16[24,768]{1,0:T(8,128)(2,1)} %get-tuple-element.62), channel_id=1, source_target_pairs={{0,4},{2,6},{4,0},{6,2},{1,5},{3,7},{5,1},{7,3},{8,12},{10,14},{12... | collective-permute-start | bytes 110600 | tf_op jit(solution)/shard_map/ppermute | solution.py:239
  509.4 7.9 %collective-permute-start.44 = (f32[2,192,1]{1,0,2:T(2,128)S(1)}, f32[2,192,1]{1,0,2:T(2,128)S(1)}, u32[]{:S(2)}, u32[]{:S(2)}) collective-permute-start(f32[2,192,1]{1,0,2:T(2,128)S(1)} %bitcast.363), channel_id=1, source_target_pairs={{0,8},{8,0},{1,9},{9,1},{2,10},{10,2},{3,11},{11,3},{4,12},{12,4},... | collective-permute-start | bytes 4616 | tf_op jit(solution)/shard_map/ppermute | solution.py:239
  515.1 22.5 %collective-permute-start.33 = (bf16[192,2304]{1,0:T(8,128)(2,1)}, bf16[192,2304]{1,0:T(8,128)(2,1)}, u32[]{:S(2)}, u32[]{:S(2)}) collective-permute-start(bf16[192,2304]{1,0:T(8,128)(2,1)} %fusion.62), channel_id=1, source_target_pairs={{0,16},{16,0},{1,17},{17,1},{2,18},{18,2},{3,19},{19,3},{4,20},{20... | collective-permute-start | bytes 2654216 | tf_op jit(solution)/shard_map/ppermute | solution.py:239
  517.3 20.2 %collective-permute-start.45 = (f32[192,1]{0,1:T(1,128)S(1)}, f32[192,1]{0,1:T(1,128)S(1)}, u32[]{:S(2)}, u32[]{:S(2)}) collective-permute-start(f32[192,1]{0,1:T(1,128)S(1)} %fusion.183), channel_id=1, source_target_pairs={{0,16},{16,0},{1,17},{17,1},{2,18},{18,2},{3,19},{19,3},{4,20},{20... | collective-permute-start | bytes 2312 | tf_op jit(solution)/shard_map/ppermute | solution.py:239
  539.7 15.8 %collective-permute-start.34 = (bf16[4,24,2304]{2,1,0:T(8,128)(2,1)S(1)}, bf16[4,24,2304]{2,1,0:T(8,128)(2,1)S(1)}, u32[]{:S(2)}, u32[]{:S(2)}) collective-permute-start(bf16[4,24,2304]{2,1,0:T(8,128)(2,1)S(1)} %fusion.110), channel_id=1, source_target_pairs={{0,1},{1,0},{2,3},{3,2},{4,5},{5,4},{6,7},{7,6},{8,9},{9,8},{10,11... | collective-permute-start | bytes 1327112 | tf_op jit(solution)/shard_map/ppermute | solution.py:239
  540.3 11.3 %collective-permute-start.46 = (f32[4,24,1]{1,0,2:T(4,128)S(1)}, f32[4,24,1]{1,0,2:T(4,128)S(1)}, u32[]{:S(2)}, u32[]{:S(2)}) collective-permute-start(f32[4,24,1]{1,0,2:T(4,128)S(1)} %bitcast.364), channel_id=1, source_target_pairs={{0,1},{1,0},{2,3},{3,2},{4,5},{5,4},{6,7},{7,6},{8,9},{9,8},{10,11... | collective-permute-start | bytes 1160 | tf_op jit(solution)/shard_map/ppermute | solution.py:239
  551.6 7.9 %collective-permute-start.47 = (f32[24,1]{0,1:T(1,128)S(1)}, f32[24,1]{0,1:T(1,128)S(1)}, u32[]{:S(2)}, u32[]{:S(2)}) collective-permute-start(f32[24,1]{0,1:T(1,128)S(1)} %get-tuple-element.79), channel_id=1, source_target_pairs={{0,2},{2,4},{4,6},{6,0},{1,3},{3,5},{5,7},{7,1},{8,10},{10,12},{12... | collective-permute-start | bytes 296 | tf_op jit(solution)/shard_map/ppermute | solution.py:239
  551.7 9.0 %collective-permute-start.49 = (f32[24,1]{0,1:T(1,128)S(1)}, f32[24,1]{0,1:T(1,128)S(1)}, u32[]{:S(2)}, u32[]{:S(2)}) collective-permute-start(f32[24,1]{0,1:T(1,128)S(1)} %get-tuple-element.80), channel_id=1, source_target_pairs={{0,6},{2,0},{4,2},{6,4},{1,7},{3,1},{5,3},{7,5},{8,14},{10,8},{12,... | collective-permute-start | bytes 296 | tf_op jit(solution)/shard_map/ppermute | solution.py:239
  555.5 5.2 collective-permute-start.48
  555.7 7.5 %collective-permute-start.35 = (bf16[24,2304]{1,0:T(8,128)(2,1)S(1)}, bf16[24,2304]{1,0:T(8,128)(2,1)S(1)}, u32[]{:S(2)}, u32[]{:S(2)}) collective-permute-start(bf16[24,2304]{1,0:T(8,128)(2,1)S(1)} %get-tuple-element.40), channel_id=1, source_target_pairs={{0,2},{2,4},{4,6},{6,0},{1,3},{3,5},{5,7},{7,1},{8,10},{10,12},{12... | collective-permute-start | bytes 331784 | tf_op jit(solution)/shard_map/ppermute | solution.py:239
  556.3 6.9 %collective-permute-start.37 = (bf16[24,2304]{1,0:T(8,128)(2,1)S(1)}, bf16[24,2304]{1,0:T(8,128)(2,1)S(1)}, u32[]{:S(2)}, u32[]{:S(2)}) collective-permute-start(bf16[24,2304]{1,0:T(8,128)(2,1)S(1)} %get-tuple-element.41), channel_id=1, source_target_pairs={{0,6},{2,0},{4,2},{6,4},{1,7},{3,1},{5,3},{7,5},{8,14},{10,8},{12,... | collective-permute-start | bytes 331784 | tf_op jit(solution)/shard_map/ppermute | solution.py:239
  559.6 8.3 %collective-permute-start.36 = (bf16[24,2304]{1,0:T(8,128)(2,1)S(1)}, bf16[24,2304]{1,0:T(8,128)(2,1)S(1)}, u32[]{:S(2)}, u32[]{:S(2)}) collective-permute-start(bf16[24,2304]{1,0:T(8,128)(2,1)S(1)} %get-tuple-element.42), channel_id=1, source_target_pairs={{0,4},{2,6},{4,0},{6,2},{1,5},{3,7},{5,1},{7,3},{8,12},{10,14},{12... | collective-permute-start | bytes 331784 | tf_op jit(solution)/shard_map/ppermute | solution.py:239
  (82 other events, 609.9 us)

commit v2 on v1

v2 whole, which is shorter than its diff:
```python
import functools

import jax
import jax.numpy as jnp
from jax import lax
from jax.experimental import pallas as pl
from jax.experimental.pallas import tpu as pltpu
from jax.sharding import Mesh, PartitionSpec as P

D = 768
HEADS = 12
HEAD_DIM = 64
GROUP_HEADS = 3
HEAD_GROUPS = HEADS // GROUP_HEADS
SEQ_DEV = 2
GROUPS = SEQ_DEV * HEAD_GROUPS
WIDTH = 256
BLOCK = 128

norm_epsilon = 1e-06
score_scale = 0.125
precise_mode = lax.Precision.HIGHEST
vmem_bytes = 50 * 1024 * 1024
f32 = jnp.float32
bf16 = jnp.bfloat16


def matmul(left, right):
    return jnp.dot(left, right, preferred_element_type=f32)


def contract_rows(left, right):
    return lax.dot_general(left, right, (((0,), (0,)), ((), ())), preferred_element_type=f32)


def contract_cols(left, right):
    return lax.dot_general(left, right, (((1,), (1,)), ((), ())), preferred_element_type=f32)


def skewed_table(table_row):
    wide = jnp.broadcast_to(table_row, (BLOCK, table_row.shape[1]))
    return pltpu.roll(wide, 1, 1, stride=1, stride_axis=0)


def key_rows(kv_refs, rows):
    for part, kv_ref in enumerate(kv_refs):
        count = kv_ref.shape[1]
        rows[part * count : (part + 1) * count, :] = kv_ref[...].T


def forward_kernel(parts, qs_ref, ks_ref, place_ref, table_ref, q_ref, *refs):
    kv_refs = refs[:parts]
    out_ref, full_ref, lse_ref, skew, score, weight, rows = refs[parts:]
    half = table_ref.shape[2] // 2
    own_count = kv_refs[0].shape[1]
    key_count = parts * own_count
    skew[...] = skewed_table(table_ref[0])
    key_rows(kv_refs, rows)
    blocks = WIDTH // BLOCK

    def one_tile(tile, carry):
        lanes = pl.ds(pl.multiple_of(tile * WIDTH, WIDTH), WIDTH)
        query = q_ref[:, lanes] * jnp.asarray(score_scale, bf16)
        query = jnp.concatenate([query, jnp.zeros_like(query)], axis=0)
        starts = [half + qs_ref[tile * blocks + i] for i in range(blocks)]
        top = jnp.full((8, WIDTH), -jnp.inf, f32)
        for block in range(key_count // BLOCK):
            offset = block * BLOCK
            bias = jnp.concatenate(
                [
                    skew[:, pl.ds(pl.multiple_of(start - ks_ref[block], BLOCK), BLOCK)]
                    for start in starts
                ],
                axis=1,
            )
            part = matmul(rows[offset : offset + BLOCK, :], query) + bias
            score[offset : offset + BLOCK, :] = part
            top = jnp.maximum(top, jnp.max(part.reshape(BLOCK // 8, 8, WIDTH), axis=0))
        top = jnp.max(top, axis=0, keepdims=True)
        total = jnp.zeros((8, WIDTH), f32)
        for block in range(key_count // BLOCK):
            offset = block * BLOCK
            part = jnp.exp(score[offset : offset + BLOCK, :] - top)
            total = total + jnp.sum(part.reshape(BLOCK // 8, 8, WIDTH), axis=0)
            weight[offset : offset + BLOCK, :] = part.astype(bf16)
        total = jnp.sum(total, axis=0, keepdims=True)
        blended = jnp.zeros((HEAD_DIM, WIDTH), f32)
        for part, kv_ref in enumerate(kv_refs):
            own = weight[part * own_count : (part + 1) * own_count, :]
            blended = blended + matmul(kv_ref[HEAD_DIM:, :], own)
        blended = blended / total
        full_ref[:, lanes] = blended
        for i in range(blocks):
            piece = blended[:, i * BLOCK : (i + 1) * BLOCK]
            out_ref[place_ref[tile * blocks + i]] = piece.astype(bf16)
        lse_ref[0, :, lanes] = top + jnp.log(total)
        return carry

    lax.fori_loop(0, q_ref.shape[1] // WIDTH, one_tile, 0)


def backward_kernel(
    parts, qs_ref, ks_ref, place_ref, table_ref, q_ref, full_ref, lse_ref, grad_ref, *refs
):
    kv_refs = refs[:parts]
    dq_ref = refs[parts]
    dkv_refs = refs[parts + 1 : 2 * parts + 1]
    dtable_ref, skew, dskew, rows, dkv = refs[2 * parts + 1 :]
    span = table_ref.shape[2]
    half = span // 2
    own_count = kv_refs[0].shape[1]
    key_count = parts * own_count
    skew[...] = skewed_table(table_ref[0])
    key_rows(kv_refs, rows)
    dskew[...] = jnp.zeros_like(dskew)
    dkv[...] = jnp.zeros_like(dkv)
    blocks = WIDTH // BLOCK
    step = 2 * BLOCK

    def one_tile(tile, carry):
        lanes = pl.ds(pl.multiple_of(tile * WIDTH, WIDTH), WIDTH)
        query = q_ref[:, lanes] * jnp.asarray(score_scale, bf16)
        grad = jnp.concatenate(
            [grad_ref[place_ref[tile * blocks + i]] for i in range(blocks)], axis=1
        )
        lse = lse_ref[0, :, lanes]
        delta = jnp.sum(grad.astype(f32) * full_ref[:, lanes], axis=0, keepdims=True)
        query = jnp.concatenate([query, jnp.zeros_like(query)], axis=0)
        grad = jnp.concatenate([jnp.zeros_like(grad), grad], axis=0)
        query_rows = query.T
        grad_rows = grad.T
        starts = [half + qs_ref[tile * blocks + i] for i in range(blocks)]
        dq = jnp.zeros((HEAD_DIM, WIDTH), f32)
        for offset in range(0, key_count, step):
            keys = rows[offset : offset + step, :]
            raw = matmul(keys, query)
            dprob = matmul(keys, grad)
            probs = []
            dscores = []
            for inner in range(0, step, BLOCK):
                key_start = ks_ref[(offset + inner) // BLOCK]
                own = slice(inner, inner + BLOCK)
                prob_row = []
                dscore_row = []
                for i, start in enumerate(starts):
                    here = pl.ds(pl.multiple_of(start - key_start, BLOCK), BLOCK)
                    cols = slice(i * BLOCK, (i + 1) * BLOCK)
                    prob = jnp.exp(raw[own, cols] + skew[:, here] - lse[:, cols])
                    dscore = prob * (dprob[own, cols] - delta[:, cols])
                    dskew[:, here] += dscore
                    prob_row.append(prob.astype(bf16))
                    dscore_row.append(dscore.astype(bf16))
                probs.append(jnp.concatenate(prob_row, axis=1))
                dscores.append(jnp.concatenate(dscore_row, axis=1))
            prob = jnp.concatenate(probs, axis=0)
            dscore = jnp.concatenate(dscores, axis=0)
            dkv[offset : offset + step, :] += matmul(dscore, query_rows) + matmul(prob, grad_rows)
            part, inside = divmod(offset, own_count)
            dq = dq + matmul(kv_refs[part][:HEAD_DIM, inside : inside + step], dscore)
        dq_ref[:, lanes] = (dq * score_scale).astype(bf16)
        return carry

    lax.fori_loop(0, q_ref.shape[1] // WIDTH, one_tile, 0)
    for part, dkv_ref in enumerate(dkv_refs):
        dkv_ref[...] = dkv[part * own_count : (part + 1) * own_count, :].T.astype(bf16)
    folded = dskew[...]
    count = BLOCK
    while count > 8:
        count //= 2
        folded = folded[:count] + pltpu.roll(folded[count:], span - count, 1)
    dtable_ref[0] = folded


def stack_spec(*shape):
    return pl.BlockSpec((1,) + shape, lambda head: (head, 0, 0))


def rows_spec(*shape):
    return pl.BlockSpec(shape, lambda head: (head, 0))


def place_spec(blocks):
    return pl.BlockSpec((blocks, HEAD_DIM, BLOCK), lambda head: (0, head, 0))


def attention_forward(qs, ks, place, table, query, kvs):
    count, span, parts = query.shape[1], table.shape[2], len(kvs)
    keys = parts * count
    scalars = pl.BlockSpec(memory_space=pltpu.SMEM)
    return pl.pallas_call(
        functools.partial(forward_kernel, parts),
        grid=(GROUP_HEADS,),
        in_specs=[scalars, scalars, scalars, stack_spec(1, span), rows_spec(HEAD_DIM, count)]
        + [rows_spec(2 * HEAD_DIM, count)] * parts,
        out_specs=[
            place_spec(count // BLOCK),
            rows_spec(HEAD_DIM, count),
            stack_spec(1, count),
        ],
        out_shape=[
            jax.ShapeDtypeStruct((count // BLOCK, GROUP_HEADS * HEAD_DIM, BLOCK), bf16),
            jax.ShapeDtypeStruct((GROUP_HEADS * HEAD_DIM, count), f32),
            jax.ShapeDtypeStruct((GROUP_HEADS, 1, count), f32),
        ],
        scratch_shapes=[
            pltpu.VMEM((BLOCK, span), f32),
            pltpu.VMEM((keys, WIDTH), f32),
            pltpu.VMEM((keys, WIDTH), bf16),
            pltpu.VMEM((keys, 2 * HEAD_DIM), bf16),
        ],
        compiler_params=pltpu.CompilerParams(vmem_limit_bytes=vmem_bytes),
        cost_estimate=pl.CostEstimate(
            flops=4 * GROUP_HEADS * HEAD_DIM * count * keys * 4,
            bytes_accessed=4 * GROUP_HEADS * HEAD_DIM * (count + keys) * 2,
            transcendentals=GROUP_HEADS * count * keys,
        ),
        name="attention_forward",
    )(qs, ks, place, table, query, *kvs)


def attention_backward(qs, ks, place, table, query, full, lse, grad, kvs):
    count, span, parts = query.shape[1], table.shape[2], len(kvs)
    keys = parts * count
    scalars = pl.BlockSpec(memory_space=pltpu.SMEM)
    return pl.pallas_call(
        functools.partial(backward_kernel, parts),
        grid=(GROUP_HEADS,),
        in_specs=[
            scalars,
            scalars,
            scalars,
            stack_spec(1, span),
            rows_spec(HEAD_DIM, count),
            rows_spec(HEAD_DIM, count),
            stack_spec(1, count),
            place_spec(count // BLOCK),
        ]
        + [rows_spec(2 * HEAD_DIM, count)] * parts,
        out_specs=[rows_spec(HEAD_DIM, count)]
        + [rows_spec(2 * HEAD_DIM, count)] * parts
        + [stack_spec(8, span)],
        out_shape=[jax.ShapeDtypeStruct((GROUP_HEADS * HEAD_DIM, count), bf16)]
        + [jax.ShapeDtypeStruct((GROUP_HEADS * 2 * HEAD_DIM, count), bf16)] * parts
        + [jax.ShapeDtypeStruct((GROUP_HEADS, 8, span), f32)],
        scratch_shapes=[
            pltpu.VMEM((BLOCK, span), f32),
            pltpu.VMEM((BLOCK, span), f32),
            pltpu.VMEM((keys, 2 * HEAD_DIM), bf16),
            pltpu.VMEM((keys, 2 * HEAD_DIM), f32),
        ],
        compiler_params=pltpu.CompilerParams(vmem_limit_bytes=vmem_bytes),
        cost_estimate=pl.CostEstimate(
            flops=10 * GROUP_HEADS * HEAD_DIM * count * keys * 4,
            bytes_accessed=4 * GROUP_HEADS * HEAD_DIM * (count + keys) * 4,
            transcendentals=GROUP_HEADS * count * keys,
        ),
        name="attention_backward",
    )(qs, ks, place, table, query, full, lse, grad, *kvs)


def shift(value, axis, step):
    size = lax.axis_size(axis)
    return lax.ppermute(value, axis, [(i, (i + step) % size) for i in range(size)])


def pick(value, index, dim=0):
    return lax.dynamic_index_in_dim(value, index, dim, keepdims=False)


def spread(parts, axis):
    return [parts[0]] + [shift(parts[k], axis, k) for k in range(1, len(parts))]


def give_back(parts, axis):
    return [parts[0]] + [shift(parts[k], axis, -k) for k in range(1, len(parts))]


def scatter_sum(value, axis, dim, wire=bf16):
    size = lax.axis_size(axis)
    index = lax.axis_index(axis)
    total = pick(value, index, dim)
    for k in range(1, size):
        part = pick(value, lax.rem(index + k, size), dim).astype(wire)
        total = total + shift(part, axis, k).astype(f32)
    return total


def sum_everywhere(value, axes):
    for axis in axes:
        size = lax.axis_size(axis)
        step = 1
        while step < size:
            value = value + lax.ppermute(value, axis, [(i, i ^ step) for i in range(size)])
            step *= 2
    return value


def scatter_rows(value, wire=bf16):
    ga, gb, ctx, dp = (lax.axis_size(a) for a in ("ga", "gb", "context", "dp"))
    rows, cols = value.shape
    own = rows // (ga * gb * ctx * dp)
    value = value.reshape(ga, gb, ctx * dp * own, cols)
    value = scatter_sum(value, "gb", 1, wire)
    value = scatter_sum(value, "ga", 0, wire)
    value = value.reshape(ctx, dp, own, cols)
    return scatter_sum(value, "dp", 1, wire)


def split_halves(value):
    high = value.astype(bf16)
    return high, (value - high.astype(f32)).astype(bf16)


def gelu_parts(values):
    c = 0.7978845608028654
    square = values * values
    bent = jnp.tanh(c * values * (1.0 + 0.044715 * square))
    act = 0.5 * values * (1.0 + bent)
    slope = 0.5 * (1.0 + bent) + 0.5 * values * (1.0 - bent * bent) * c * (
        1.0 + 3 * 0.044715 * square
    )
    return act, slope


def after(value, *others):
    return lax.optimization_barrier((value,) + others)[0]


def add_up(parts):
    total = parts[0].astype(f32)
    for part in parts[1:]:
        total = total + part.astype(f32)
    return total


def exchange(value, axis):
    return lax.all_to_all(value, axis, 0, 0, tiled=True)


def local(
    tokens,
    cotangent,
    query_key_value_weight,
    output_weight,
    gain_one,
    gain_two,
    router_weight,
    w_in,
    w_down,
    position_bias,
    bucket,
    route,
    slot,
    dropped,
):
    seq_count, tok_count = tokens.shape[:2]
    row_count = seq_count * tok_count
    ga, gb, ctx, dp = (lax.axis_size(a) for a in ("ga", "gb", "context", "dp"))
    experts = ga * gb
    capacity = (5 * row_count + 4 * experts - 1) // (4 * experts)
    group_rows = GROUPS * tok_count
    expert_axis = ("ga", "gb")
    group_axis = ("ga", "context")
    ga_index, gb_index = lax.axis_index("ga"), lax.axis_index("gb")
    ctx_index, dp_index = lax.axis_index("context"), lax.axis_index("dp")
    group_index = lax.axis_index(group_axis)
    head_group = lax.rem(group_index, HEAD_GROUPS)
    in_order = tok_count % BLOCK != 0

    picked = {}

    def group_perm(dga, dz):
        flat = []
        for a in range(ga):
            for z in range(ctx):
                flat.append((a * ctx + z, (a + dga) % ga * ctx + (z + dz) % ctx))
        return flat

    steps = [(dga, dz) for dga in range(ga) for dz in range(ctx)]

    def sequence_at(dga, dz):
        key = dga if ctx == HEAD_GROUPS else (dga, dz)
        if key not in picked:
            to_ga = lax.rem(ga_index + dga, ga)
            to_ctx = 0 if ctx == HEAD_GROUPS else lax.rem(ctx_index + dz, ctx)
            picked[key] = pick(tokens, (to_ga * ctx + to_ctx) // HEAD_GROUPS)
        return picked[key]

    token_blocks = [
        sequence_at(*step)
        if step == (0, 0)
        else lax.ppermute(sequence_at(*step), group_axis, group_perm(*step))
        for step in steps
    ]
    source_ga = [lax.rem(ga_index - dga + ga, ga) for dga, dz in steps]
    source_ctx = [lax.rem(ctx_index - dz + ctx, ctx) for dga, dz in steps]
    source = jnp.stack([a * ctx + z for a, z in zip(source_ga, source_ctx)]).astype(jnp.int32)
    if in_order:
        group_tokens = jnp.concatenate(token_blocks, axis=0).reshape(GROUPS, tok_count, D)
        group_tokens = group_tokens[jnp.argsort(source)].reshape(group_rows, D)
        place = jnp.arange(group_rows // BLOCK, dtype=jnp.int32)
    else:
        group_tokens = jnp.concatenate(token_blocks, axis=0)
        place = jnp.repeat(source, tok_count // BLOCK) * (tok_count // BLOCK) + jnp.tile(
            jnp.arange(tok_count // BLOCK, dtype=jnp.int32), GROUPS
        )
    per_span = ctx * tok_count // BLOCK

    def begins(core):
        return ((place // per_span * gb + core) * per_span + place % per_span) * BLOCK

    query_starts = begins(gb_index)
    key_starts = jnp.concatenate(
        [begins(lax.rem(gb_index - k + gb, gb)) for k in range(gb)]
    ).astype(jnp.int32)

    weight_group = query_key_value_weight.T.reshape(3, HEAD_GROUPS, GROUP_HEADS, HEAD_DIM, D)
    weight_group = pick(weight_group, head_group, 1)
    weight_query = weight_group[0].reshape(GROUP_HEADS * HEAD_DIM, D)
    weight_kv = jnp.transpose(weight_group[1:], (1, 0, 2, 3)).reshape(-1, D)

    route_flat = route.reshape(-1)
    position = route_flat * capacity + slot.reshape(-1)
    assign = (
        (jnp.arange(experts * capacity, dtype=jnp.int32)[:, None] == position[None, :])
        & (dropped.reshape(-1) == 0)[None, :]
    ).astype(bf16)
    grad_low = cotangent.reshape(row_count, D)
    grad_buffer = matmul(assign, grad_low).astype(bf16).reshape(experts, capacity, D)
    grad_rows = exchange(grad_buffer, expert_axis).reshape(-1, D)

    onehot = (
        jnp.arange(position_bias.shape[0], dtype=jnp.int32)[:, None]
        == jnp.pad(bucket[::-1], (0, 1), constant_values=-1)[None, :]
    ).astype(f32)
    bias_heads = lax.dynamic_slice_in_dim(position_bias.T, head_group * GROUP_HEADS, GROUP_HEADS, 0)
    table = jnp.dot(bias_heads, onehot, precision=precise_mode, preferred_element_type=f32)
    table = table[:, None, :]

    def normalised(values):
        scale = lax.rsqrt(jnp.mean(values * values, axis=-1, keepdims=True) + norm_epsilon)
        return scale, values * scale

    group_normed = (normalised(group_tokens.astype(f32))[1] * gain_one).astype(bf16)
    own_kv = contract_cols(weight_kv, group_normed).astype(bf16)
    kvs = [own_kv] + [shift(own_kv, "gb", k) for k in range(1, gb)]
    query = contract_cols(weight_query, group_normed).astype(bf16)

    early = [k for k in range(1, ctx) if k == ctx // 2]
    late = [k for k in range(1, ctx) if k != ctx // 2]
    grad_blocks = {0: grad_rows}
    first_rows = after(grad_rows, group_tokens)
    for k in early:
        grad_blocks[k] = shift(first_rows, "context", k)

    attended_parts, attended, lse = attention_forward(
        query_starts, key_starts, place, table, query, kvs
    )

    def to_sources(parts):
        parts = parts.reshape(group_rows // BLOCK, -1, BLOCK)
        if in_order:
            parts = jnp.transpose(
                parts.reshape(group_rows // BLOCK, parts.shape[1], BLOCK // tok_count, tok_count),
                (0, 2, 1, 3),
            ).reshape(GROUPS, parts.shape[1], tok_count)
        return parts

    def from_sources(parts):
        if in_order:
            merged = BLOCK // tok_count
            parts = jnp.transpose(
                parts.reshape(GROUPS // merged, merged, parts.shape[1], tok_count), (0, 2, 1, 3)
            ).reshape(GROUPS // merged, parts.shape[1], BLOCK)
        return parts

    attended_low = exchange(to_sources(attended_parts), group_axis)
    attended_low = attended_low.reshape(seq_count, D, tok_count)
    second_rows = after(grad_rows, attended_low)
    for k in late:
        grad_blocks[k] = shift(second_rows, "context", k)

    inputs = tokens.reshape(row_count, D).astype(f32)
    branch = jnp.concatenate(
        [contract_rows(attended_low[i], output_weight) for i in range(seq_count)], axis=0
    )
    middle = inputs + branch
    scale_two, unit_two = normalised(middle)
    normalized_second = unit_two * gain_two
    router_logits = jnp.dot(
        normalized_second, router_weight, precision=precise_mode, preferred_element_type=f32
    )
    router = jax.nn.softmax(router_logits, axis=-1)
    chosen = (route_flat[:, None] == jnp.arange(experts, dtype=jnp.int32)[None, :]).astype(f32)
    gate = jnp.sum(router * chosen, axis=-1, keepdims=True)

    gate_high, gate_low = split_halves(gate)
    payload = jnp.concatenate(
        [
            normalized_second.astype(bf16),
            gate_high,
            gate_low,
            jnp.zeros((row_count, 126), bf16),
        ],
        axis=1,
    )
    buffer = matmul(assign, payload).astype(bf16).reshape(experts, capacity, D + 128)
    received = exchange(buffer, expert_axis).reshape(-1, D + 128)
    row_blocks = spread([received[:, :D]] * ctx, "context")

    local_in = w_in[0]
    local_down = w_down[0]
    ones = jnp.ones((8, local_in.shape[1]), bf16)
    hidden_blocks, pre_blocks, back_parts, gate_parts = [], [], [], []
    for k in range(ctx):
        grad_hidden = matmul(after(grad_blocks[k], received), local_down)
        act, slope = gelu_parts(matmul(row_blocks[k], local_in))
        hidden = act.astype(bf16)
        grad_pre = grad_hidden * slope
        hidden_blocks.append(hidden)
        pre_blocks.append(grad_pre.astype(bf16))
        back_parts.append(contract_cols(pre_blocks[k], local_in).astype(bf16))
        gate_parts.append(contract_cols(ones, (grad_hidden * hidden.astype(f32)).astype(bf16)))

    back_sum = add_up(give_back(back_parts, "context")).astype(bf16)
    gate_sum = add_up(give_back(gate_parts, "context"))
    gate_halves = split_halves(gate_sum[:1])
    gate_column = contract_rows(
        jnp.concatenate(gate_halves + (jnp.zeros((6, gate_sum.shape[1]), bf16),), axis=0),
        jnp.eye(8, 128, dtype=bf16),
    ).astype(bf16)
    back_rows = jnp.concatenate([back_sum, gate_column], axis=1)
    back_rows = exchange(back_rows.reshape(experts, capacity, D + 128), expert_axis)
    back_rows = contract_rows(assign, back_rows.reshape(-1, D + 128))
    grad_sent = back_rows[:, :D] * gate
    grad_gate = back_rows[:, D : D + 1] + back_rows[:, D + 1 : D + 2]

    grad_out = grad_low.astype(f32)
    grad_logits = grad_gate * gate * (chosen - router)
    grad_normed_two = grad_sent + lax.dot_general(
        grad_logits,
        router_weight,
        (((1,), (1,)), ((), ())),
        precision=precise_mode,
        preferred_element_type=f32,
    )
    scaled_two = gain_two * grad_normed_two
    cube_two = scale_two * scale_two * scale_two
    grad_middle = (
        grad_out
        + scale_two * scaled_two
        - middle * cube_two * jnp.mean(scaled_two * middle, axis=-1, keepdims=True)
    )
    grad_branch = grad_middle.astype(bf16)

    grad_heads = jnp.concatenate(
        [
            contract_cols(output_weight, grad_branch[i * tok_count : (i + 1) * tok_count])
            for i in range(seq_count)
        ],
        axis=0,
    ).astype(bf16)
    grad_heads = exchange(
        grad_heads.reshape(GROUPS, GROUP_HEADS * HEAD_DIM, tok_count), group_axis
    )

    def out_part(k, *others):
        return contract_cols(after(hidden_blocks[k], *others), local_down).astype(bf16)

    result_parts = {0: out_part(0, back_sum)}
    for k in early:
        result_parts[k] = shift(out_part(k, back_sum), "context", -k)
    for k in late:
        result_parts[k] = shift(after(out_part(k, back_sum), grad_heads), "context", -k)
    gate_rows = after(received[:, D:], back_sum)
    gate_blocks = spread([gate_rows] * ctx, "context")

    outs = attention_backward(
        query_starts,
        key_starts,
        place,
        table,
        query,
        attended,
        lse,
        from_sources(grad_heads),
        kvs,
    )
    grad_query, grad_kvs, grad_table = outs[0], outs[1:-1], outs[-1]
    grad_kv = add_up(give_back(grad_kvs, "gb")).astype(bf16)
    grad_projected = jnp.concatenate([grad_query, grad_kv], axis=0)
    weight_all = jnp.concatenate([weight_query, weight_kv], axis=0)
    part_normed = contract_rows(grad_projected, weight_all).astype(bf16)
    part_normed = part_normed.reshape(GROUPS, tok_count, D)
    if in_order:
        part_normed = part_normed[source]
    returned_normed = [
        part_normed[0]
        if step == (0, 0)
        else lax.ppermute(
            part_normed[i], group_axis, [(b, a) for a, b in group_perm(*step)]
        )
        for i, step in enumerate(steps)
    ]
    sums = [0.0] * seq_count
    for (dga, dz), part in zip(steps, returned_normed):
        from_ga = lax.rem(ga_index + dga, ga)
        from_ctx = lax.rem(ctx_index + dz, ctx)
        of_sequence = (from_ga * ctx + from_ctx) // HEAD_GROUPS
        for i in range(seq_count):
            sums[i] = sums[i] + jnp.where(of_sequence == i, part.astype(f32), 0.0)
    grad_normed = jnp.concatenate(sums, axis=0)
    scale_one = normalised(inputs)[0]
    scaled_one = gain_one * grad_normed
    cube_one = scale_one * scale_one * scale_one
    grad_inputs = (
        grad_middle
        + scale_one * scaled_one
        - inputs * cube_one * jnp.mean(scaled_one * inputs, axis=-1, keepdims=True)
    )

    qkv_part = lax.dot_general(
        group_normed, grad_projected, (((0,), (1,)), ((), ())), preferred_element_type=f32
    )
    own_rows = D // (ga * gb * ctx * dp)
    qkv_part = scatter_rows(qkv_part)
    by_group = [0.0] * HEAD_GROUPS
    for k in range(ctx):
        part = pick(qkv_part, lax.rem(ctx_index + k, ctx))
        if k:
            part = shift(part.astype(bf16), "context", k)
        by_group[k % HEAD_GROUPS] = by_group[k % HEAD_GROUPS] + part.astype(f32)
    by_group = jnp.stack(by_group)
    order = lax.rem(
        ctx_index - jnp.arange(HEAD_GROUPS, dtype=jnp.int32) + 2 * HEAD_GROUPS, HEAD_GROUPS
    )
    by_group = jnp.stack([pick(by_group, order[i]) for i in range(HEAD_GROUPS)], axis=1)
    width = GROUP_HEADS * HEAD_DIM
    query_cols = by_group[:, :, :width].reshape(own_rows, 1, D)
    kv_cols = by_group[:, :, width:].reshape(own_rows, HEADS, 2, HEAD_DIM)
    kv_cols = jnp.transpose(kv_cols, (0, 2, 1, 3)).reshape(own_rows, 2, D)
    qkv_total = jnp.concatenate([query_cols, kv_cols], axis=1).reshape(own_rows, 3 * D)
    first_row = (lax.axis_index(("ga", "gb", "context", "dp"))) * own_rows
    weight_rows = lax.dynamic_slice_in_dim(query_key_value_weight, first_row, own_rows, 0)
    gain_rows = lax.dynamic_slice_in_dim(gain_one, first_row, own_rows, 0)
    gain_one_total = jnp.sum(qkv_total * weight_rows.astype(f32), axis=1) / gain_rows

    result = add_up([result_parts[k] for k in range(ctx)]).astype(bf16)
    returned_rows = exchange(result.reshape(experts, capacity, D), expert_axis).reshape(-1, D)
    returned = contract_rows(assign, returned_rows)
    output = (middle + gate * returned).astype(bf16)

    all_rows = jnp.concatenate(row_blocks, axis=0)
    all_grads = jnp.concatenate([grad_blocks[k] for k in range(ctx)], axis=0)
    all_gates = jnp.concatenate(gate_blocks, axis=0)[:, :2].astype(f32)
    all_gates = all_gates[:, :1] + all_gates[:, 1:2]
    all_gates = after(all_gates, grad_query)
    all_hidden = jnp.concatenate(hidden_blocks, axis=0)
    all_pre = (jnp.concatenate(pre_blocks, axis=0).astype(f32) * all_gates).astype(bf16)
    all_returned = (all_gates * all_grads.astype(f32)).astype(bf16)
    down_part = contract_rows(all_returned, all_hidden)
    in_part = contract_rows(all_rows, all_pre)
    in_grad = scatter_sum(in_part.reshape(D, dp, -1), "dp", 1)
    down_grad = scatter_sum(down_part.reshape(D, dp, -1), "dp", 1)

    late_branch = after(grad_branch, grad_heads)
    out_part_grad = add_up(
        [
            matmul(attended_low[i], late_branch[i * tok_count : (i + 1) * tok_count])
            for i in range(seq_count)
        ]
    )
    router_grad = lax.dot_general(
        normalized_second,
        grad_logits,
        (((0,), (0,)), ((), ())),
        precision=precise_mode,
        preferred_element_type=f32,
    )
    gain_two_grad = jnp.sum(grad_normed_two * unit_two, axis=0)
    dense = jnp.concatenate(
        [out_part_grad, router_grad, gain_two_grad[:, None], jnp.zeros((D, 123), f32)], axis=1
    )
    dense = scatter_sum(scatter_rows(dense), "context", 0)
    span = bucket.shape[0]
    grad_table = jnp.pad(grad_table, ((0, 0), (0, 0), (0, 8)))
    by_offset = grad_table[:, 0, 1 : 1 + span]
    for r in range(1, 8):
        by_offset = by_offset + grad_table[:, r, r + 1 : r + 1 + span]
    bias_part = lax.dot_general(
        by_offset,
        onehot[:, :span],
        (((1,), (1,)), ((), ())),
        precision=precise_mode,
        preferred_element_type=f32,
    )
    bias_grad = lax.dynamic_update_slice_in_dim(
        jnp.zeros((HEADS, bias_part.shape[1]), f32), bias_part, head_group * GROUP_HEADS, 0
    )
    bias_grad = sum_everywhere(bias_grad, ("gb", "ga", "dp", "context")).T
    return (
        output.reshape(seq_count, tok_count, D),
        grad_inputs.astype(bf16).reshape(seq_count, tok_count, D),
        qkv_total,
        dense[:, :D],
        gain_one_total,
        dense[:, D + 4],
        dense[:, D : D + 4],
        in_grad[None],
        down_grad[None],
        bias_grad,
    )


def solution(mesh):
    ctx = mesh.shape["context"]
    ga = max(GROUPS // ctx, 1)
    gb = mesh.shape["expert"] // ga
    fine = Mesh(
        mesh.devices.reshape(ga, gb, ctx, mesh.shape["dp"]), ("ga", "gb", "context", "dp")
    )
    expert = ("ga", "gb")
    blocks = ("ga", "gb", "context")
    everywhere = ("ga", "gb", "context", "dp")
    return jax.shard_map(
        local,
        mesh=fine,
        in_specs=(
            P("dp", blocks, None),
            P("dp", blocks, None),
            P(),
            P(),
            P(),
            P(),
            P(),
            P(expert, None, "context"),
            P(expert, None, "context"),
            P(),
            P(),
            P("dp", blocks),
            P("dp", blocks),
            P("dp", blocks),
        ),
        out_specs=(
            P("dp", blocks, None),
            P("dp", blocks, None),
            P(everywhere, None),
            P(everywhere, None),
            P(everywhere),
            P(everywhere),
            P(everywhere, None),
            P(expert, None, ("context", "dp")),
            P(expert, None, ("context", "dp")),
            P(),
        ),
        check_vma=False,
    )
```

time: 580 us -> 470 us (0.81)
  local copies, waits for them, and re-layouts: 126 us -> 51.7 us
  waiting for transfers between devices: 198 us -> 158 us
  between operations: 2.17 us -> 10.9 us
    ppermute x61 -> x34, waiting for transfers between devices: 160 us -> 82 us  [shift(): lax.ppermute(value, axis, [(i, (i + step) % size) for i in range(size)])]
    ppermute x61 -> x34, starting transfers between devices: 81 us -> 46.6 us  [shift(): lax.ppermute(value, axis, [(i, (i + step) % size) for i in range(size)])]
    ppermute x0 -> x14, starting transfers between devices: none -> 26.1 us  [the longest x7 13.8 us: local(): lax.ppermute(sequence_at(*step), group_axis, group_perm(*step))]
    reshape x12 -> x4, local copies, waits for them, and re-layouts: 25.9 us -> 0.45 us  [the longest x1 0.22 us: local(): kv_cols = by_group[:, :, width:].reshape(own_rows, HEADS, 2, HEAD_DIM)]
    ppermute x0 -> x14, waiting for transfers between devices: none -> 24.9 us  [the longest x7 17.7 us: local(): lax.ppermute(part_normed[i], group_axis, [(b, a) for a, b in group_perm(*...]
    unnamed x171 -> x183, local copies, waits for them, and re-layouts: 39 us -> 22.7 us
    add x15 -> x7, other arithmetic: 13.2 us -> 1.5 us  [scatter_sum(): total = total + shift(part, axis, k).astype(f32)]
    all_to_all x4 -> x6, waiting for transfers between devices: 32.7 us -> 43.8 us  [exchange(): return lax.all_to_all(value, axis, 0, 0, tiled=True)]
  transfers between devices with their start and end apart: 70 -> 59, of which waited for: 25 -> 21; matrix products, arithmetic and copies ran while one was open for 28% -> 28% of each run, Pallas kernels for 8% -> 11%
where the time goes in v2:
time: 470 us; the launch traced here: 460 us
  waiting for transfers between devices  158 us (34%)
  starting transfers between devices  101 us (21%)
  matrix products  55.8 us (12%)
  local copies, waits for them, and re-layouts  51.7 us (11%)
  Pallas kernels  50.6 us (11%)
  other arithmetic  32.5 us (7%)
  between operations  10.9 us (2%)
    ppermute x34, waiting for transfers between devices, shift(): lax.ppermute(value, axis, [(i, (i + step) % size) for i in range(size)])  82 us
    ppermute x34, starting transfers between devices, shift(): lax.ppermute(value, axis, [(i, (i + step) % size) for i in range(size)])  46.6 us
    all_to_all x6, waiting for transfers between devices, exchange(): return lax.all_to_all(value, axis, 0, 0, tiled=True)  43.8 us
    pallas_call x1, Pallas kernels, attention_backward(): pl.pallas_call(functools.partial(backward_kernel, parts), grid=(GROUP_HEA...  30.9 us
    all_to_all x6, starting transfers between devices, exchange(): return lax.all_to_all(value, axis, 0, 0, tiled=True)  27.1 us
    unnamed x183, local copies, waits for them, and re-layouts  22.7 us
    pallas_call x1, Pallas kernels, attention_forward(): pl.pallas_call(functools.partial(forward_kernel, parts), grid=(GROUP_HEAD...  19.7 us
    dot_general x12, matrix products, matmul(): return jnp.dot(left, right, preferred_element_type=f32)  19.5 us
  transfers between devices with their start and end apart: 59, of which 21 were waited for; matrix products, arithmetic and copies ran while one was open for 28% of the time, Pallas kernels for 11%

profile of v2, /device:TPU:0, one launch (start us, length us, event | category | flops | bytes accessed | tf_op | source)
XLA Modules:
  0.0 460.4 jit_solution(15487857765880151408)
XLA Ops:
  0.7 1.7 constant_dynamic-update-slice_fusion.7
  2.4 3.0 collective-permute-start
  5.4 2.6 collective-permute-start.1
  13.9 2.1 convolution_convert_fusion.3
  16.0 4.1 all-to-all-start.2
  20.2 5.8 %copy.76 = bf16[768,2304]{0,1:T(8,128)(2,1)} copy(bf16[768,2304]{1,0:T(8,128)(2,1)} %param.16) | data formatting | bytes 7077888 | tf_op args[2]
  32.2 1.8 collective-permute-start.5
  34.0 2.9 collective-permute-start.6
  38.8 7.2 %collective-permute-done.5 = bf16[128,768]{1,0:T(8,128)(2,1)S(1)} collective-permute-done((bf16[128,768]{1,0:T(8,128)(2,1)S(1)}, bf16[128,768]{1,0:T(8,128)(2,1)S(1)}, u32[]{:S(2)}, u32[]{:S(2)}) %collective-permute-start.5) | collective-permute-done | bytes 196640 | tf_op jit(solution)/shard_map/ppermute | solution.py:392
  61.3 2.3 convolution_convert_fusion.12.q_ref
  63.6 19.7 %attention_forward.1 = (bf16[8,192,128]{2,1,0:T(8,128)(2,1)}, f32[192,1024]{1,0:T(8,128)S(1)}, f32[3,1,1024]{2,1,0:T(1,128)S(1)}) custom-call(s32[8]{0:T(128)S(1)} %get-tuple-element.137.qs_ref, s32[16]{0:T(128)S(1)} %pad_add_fusion.ks_ref, s32[8]{0:T(128)S(1)} %stack.72.place_ref, f32[3,1,4096]{2,1,0:T(1,128)S(1)} %broadcast_in_dim.62.table_ref, ...), custom_call_target="tpu_custom_call" | custom-call | flops 6442450944 | bytes 4718592 | tf_op jit(solution)/shard_map/attention_forward/pallas_call | solution.py:190
  84.2 7.5 %all-to-all-start = ((bf16[8,192,128]{2,1,0:T(8,128)(2,1)}), bf16[8,192,128]{2,1,0:T(8,128)(2,1)}, u32[]{:S(2)}, u32[]{:S(2)}) async-start(bf16[8,192,128]{2,1,0:T(8,128)(2,1)} %get-tuple-element.31), calls=%async_computation | async-start | bytes 786432 | tf_op jit(solution)/shard_map/all_to_all | solution.py:337
  91.7 2.1 collective-permute-start.8
  93.8 1.9 collective-permute-start.14
  96.7 19.5 %all-to-all-done = bf16[8,192,128]{2,1,0:T(8,128)(2,1)} async-done(((bf16[8,192,128]{2,1,0:T(8,128)(2,1)}), bf16[8,192,128]{2,1,0:T(8,128)(2,1)}, u32[]{:S(2)}, u32[]{:S(2)}) %all-to-all-start) | async-done | bytes 393248 | tf_op jit(solution)/shard_map/all_to_all | solution.py:337
  123.2 2.3 convolution_convert_fusion.2
  125.6 4.2 all-to-all-start.1
  132.0 7.2 %all-to-all-done.1 = bf16[4,80,896]{2,1,0:T(8,128)(2,1)} async-done(((bf16[4,80,896]{2,1,0:T(8,128)(2,1)}), bf16[4,80,896]{2,1,0:T(8,128)(2,1)}, u32[]{:S(2)}, u32[]{:S(2)}) %all-to-all-start.1) | async-done | bytes 573472 | tf_op jit(solution)/shard_map/all_to_all | solution.py:337
  141.6 3.7 collective-permute-start.15
  145.3 22.8 %collective-permute-done.11 = bf16[320,768]{1,0:T(8,128)(2,1)} collective-permute-done((bf16[320,768]{1,0:T(8,128)(2,1)}, bf16[320,768]{1,0:T(8,128)(2,1)}, u32[]{:S(2)}, u32[]{:S(2)}) %collective-permute-start.11) | collective-permute-done | bytes 491552 | tf_op jit(solution)/shard_map/ppermute | solution.py:263
  168.0 2.0 fusion.51
  173.2 2.0 multiply_convert_fusion.15
  175.5 1.7 fusion.45
  181.9 11.2 %collective-permute-start.19 = (f32[8,320]{1,0:T(8,128)S(1)}, f32[8,320]{1,0:T(8,128)S(1)}, u32[]{:S(2)}, u32[]{:S(2)}) collective-permute-start(f32[8,320]{1,0:T(8,128)S(1)} %fusion.89), channel_id=1, source_target_pairs={{0,2},{2,4},{4,6},{6,0},{1,3},{3,5},{5,7},{7,1},{8,10},{10,12},{12... | collective-permute-start | bytes 30728 | tf_op jit(solution)/shard_map/ppermute | solution.py:263
  197.5 9.4 %collective-permute-done.10 = bf16[320,768]{1,0:T(8,128)(2,1)S(1)} collective-permute-done((bf16[320,768]{1,0:T(8,128)(2,1)S(1)}, bf16[320,768]{1,0:T(8,128)(2,1)S(1)}, u32[]{:S(2)}, u32[]{:S(2)}) %collective-permute-start.10) | collective-permute-done | bytes 491552 | tf_op jit(solution)/shard_map/ppermute | solution.py:263
  206.9 30.8 %collective-permute-done.13 = bf16[320,768]{1,0:T(8,128)(2,1)S(1)} collective-permute-done((bf16[320,768]{1,0:T(8,128)(2,1)S(1)}, bf16[320,768]{1,0:T(8,128)(2,1)S(1)}, u32[]{:S(2)}, u32[]{:S(2)}) %collective-permute-start.13) | collective-permute-done | bytes 491552 | tf_op jit(solution)/shard_map/ppermute | solution.py:263
  238.5 1.7 collective-permute-start.44
  240.2 2.8 collective-permute-start.45
  243.9 3.7 all-to-all-start.3
  247.6 2.4 convolution_convert_fusion.6
  254.1 1.8 fusion.114
  262.2 3.6 all-to-all-start.4
  269.4 16.1 %all-to-all-done.4.grad_ref = bf16[8,192,128]{2,1,0:T(8,128)(2,1)S(1)} async-done(((bf16[8,192,128]{2,1,0:T(8,128)(2,1)}), bf16[8,192,128]{2,1,0:T(8,128)(2,1)S(1)}, u32[]{:S(2)}, u32[]{:S(2)}) %all-to-all-start.4) | async-done | bytes 393248 | tf_op jit(solution)/shard_map/all_to_all | solution.py:337
  286.6 30.9 %attention_backward.1 = (bf16[192,1024]{1,0:T(8,128)(2,1)S(1)}, bf16[384,1024]{1,0:T(8,128)(2,1)S(1)}, bf16[384,1024]{1,0:T(8,128)(2,1)S(1)}, f32[3,8,4096]{2,1,0:T(8,128)S(1)}) custom-call(s32[8]{0:T(128)S(1)} %get-tuple-element.137.qs_ref, s32[16]{0:T(128)S(1)} %pad_add_fusion.ks_ref, s32[8]{0:T(128)S(1)} %stack.72.place_ref, ...), custom_call_target="tpu_custom_call" | custom-call | flops 16106127360 | bytes 9437184 | tf_op jit(solution)/shard_map/attention_backward/pallas_call | solution.py:225
  322.1 3.8 fusion.4
  326.9 2.1 copy.101
  332.1 2.2 collective-permute-start.22
  334.4 4.7 %fusion.3 = f32[768,768]{0,1:T(8,128)} fusion(bf16[320,768]{1,0:T(8,128)(2,1)S(1)} %copy-done.78, bf16[320,768]{1,0:T(8,128)(2,1)S(1)} %copy-done.76, bf16[320,768]{1,0:T(8,128)(2,1)S(1)} %copy-done.74, bf16[320,768]{1,0:T(8,128)(2,1)S(1)} %copy-done.43, bf16[320,768]{1,0:T(8,128)(2,1)} %copy-done.84, bf16[320,768]{1,0:T(8,128)(2,1)} %copy-done.83, ...), kind=kOutput, calls=%fused_computation.8 | convolution fusion | flops 1527644160 | bytes 6296576 | tf_op jit(solution)/shard_map/dot_general | solution.py:33
  339.0 1.8 convolution_add_fusion
  343.3 2.3 maximum_maximum_fusion
  349.2 1.9 collective-permute-done.50
  352.1 4.2 collective-permute-done.51
  358.6 2.7 copy.91
  361.4 2.1 copy.100
  365.4 2.9 add_convert_fusion.1
  368.2 4.1 all-to-all-start.5
  372.4 2.6 fusion.39
  375.0 3.5 collective-permute-done.46
  378.5 2.2 fusion.40
  386.6 2.7 collective-permute-start.24
  389.3 1.7 fusion.79
  391.0 2.0 collective-permute-start.26
  393.7 2.6 collective-permute-start.28
  397.3 4.3 collective-permute-start.29
  401.5 12.1 %collective-permute-done.25 = bf16[128,768]{1,0:T(8,128)(2,1)S(1)} collective-permute-done((bf16[128,768]{1,0:T(8,128)(2,1)S(1)}, bf16[128,768]{1,0:T(8,128)(2,1)S(1)}, u32[]{:S(2)}, u32[]{:S(2)}) %collective-permute-start.25) | collective-permute-done | bytes 196640 | tf_op jit(solution)/shard_map/ppermute | solution.py:600
  413.6 2.3 fusion.38
  417.2 5.7 %collective-permute-done.29 = bf16[128,768]{1,0:T(8,128)(2,1)S(1)} collective-permute-done((bf16[128,768]{1,0:T(8,128)(2,1)}, bf16[128,768]{1,0:T(8,128)(2,1)S(1)}, u32[]{:S(2)}, u32[]{:S(2)}) %collective-permute-start.29) | collective-permute-done | bytes 196640 | tf_op jit(solution)/shard_map/ppermute | solution.py:600
  429.2 3.6 collective-permute-done.39
  433.7 2.7 collective-permute-start.41
  436.4 2.8 collective-permute-start.42
  442.3 3.4 collective-permute-done.32
  447.6 3.1 collective-permute-done.33
  452.8 1.9 collective-permute-done.36
  454.7 1.6 collective-permute-done.35
  (398 shorter events, 109.5 us)
Async XLA Ops:
  0.6 172.6 %copy-start = (bf16[1,768,768]{2,1,0:T(8,128)(2,1)S(1)}, bf16[1,768,768]{2,1,0:T(8,128)(2,1)}, u32[]{:S(2)}) copy-start(bf16[1,768,768]{2,1,0:T(8,128)(2,1)} %param.21) | copy-start | bytes 3538948
  2.4 29.8 %collective-permute-start = (bf16[128,768]{1,0:T(8,128)(2,1)}, bf16[128,768]{1,0:T(8,128)(2,1)S(1)}, u32[]{:S(2)}, u32[]{:S(2)}) collective-permute-start(bf16[128,768]{1,0:T(8,128)(2,1)} %get-tuple-element.105), channel_id=1, source_target_pairs={{0,2},{2,4},{4,6},{6,0},{16,18},{18,20},{20,22},{22,16},{1,3},{3,5... | collective-permute-start | bytes 589832 | tf_op jit(solution)/shard_map/ppermute | solution.py:392
  5.4 28.5 %collective-permute-start.1 = (bf16[128,768]{1,0:T(8,128)(2,1)}, bf16[128,768]{1,0:T(8,128)(2,1)S(1)}, u32[]{:S(2)}, u32[]{:S(2)}) collective-permute-start(bf16[128,768]{1,0:T(8,128)(2,1)} %get-tuple-element.105), channel_id=1, source_target_pairs={{0,4},{2,6},{4,0},{6,2},{16,20},{18,22},{20,16},{22,18},{1,5},{3,7... | collective-permute-start | bytes 589832 | tf_op jit(solution)/shard_map/ppermute | solution.py:392
  8.0 28.9 %collective-permute-start.2 = (bf16[128,768]{1,0:T(8,128)(2,1)}, bf16[128,768]{1,0:T(8,128)(2,1)S(1)}, u32[]{:S(2)}, u32[]{:S(2)}) collective-permute-start(bf16[128,768]{1,0:T(8,128)(2,1)} %get-tuple-element.105), channel_id=1, source_target_pairs={{0,6},{2,0},{4,2},{6,4},{16,22},{18,16},{20,18},{22,20},{1,7},{3,1... | collective-permute-start | bytes 589832 | tf_op jit(solution)/shard_map/ppermute | solution.py:392
  10.3 26.6 %collective-permute-start.3 = (bf16[128,768]{1,0:T(8,128)(2,1)S(1)}, bf16[128,768]{1,0:T(8,128)(2,1)}, u32[]{:S(2)}, u32[]{:S(2)}) collective-permute-start(bf16[128,768]{1,0:T(8,128)(2,1)S(1)} %dynamic-slice_bitcast_fusion.1), channel_id=1, source_target_pairs={{0,16},{2,18},{4,20},{6,22},{16,0},{18,2},{20,4},{22,6},{1,17},{3,... | collective-permute-start | bytes 589832 | tf_op jit(solution)/shard_map/ppermute | solution.py:392
  11.9 26.0 %collective-permute-start.4 = (bf16[128,768]{1,0:T(8,128)(2,1)S(1)}, bf16[128,768]{1,0:T(8,128)(2,1)}, u32[]{:S(2)}, u32[]{:S(2)}) collective-permute-start(bf16[128,768]{1,0:T(8,128)(2,1)S(1)} %dynamic-slice_bitcast_fusion.1), channel_id=1, source_target_pairs={{0,18},{2,20},{4,22},{6,16},{16,2},{18,4},{20,6},{22,0},{1,19},{3,... | collective-permute-start | bytes 589832 | tf_op jit(solution)/shard_map/ppermute | solution.py:392
  16.0 68.2 %all-to-all-start.2 = ((bf16[4,80,768]{2,1,0:T(8,128)(2,1)}), bf16[4,80,768]{2,1,0:T(8,128)(2,1)}, u32[]{:S(2)}, u32[]{:S(2)}) async-start(bf16[4,80,768]{2,1,0:T(8,128)(2,1)} %bitcast.29), calls=%async_computation.2 | async-start | bytes 983040 | tf_op jit(solution)/shard_map/all_to_all | solution.py:337
  32.2 13.8 %collective-permute-start.5 = (bf16[128,768]{1,0:T(8,128)(2,1)S(1)}, bf16[128,768]{1,0:T(8,128)(2,1)S(1)}, u32[]{:S(2)}, u32[]{:S(2)}) collective-permute-start(bf16[128,768]{1,0:T(8,128)(2,1)S(1)} %dynamic-slice_bitcast_fusion.1), channel_id=1, source_target_pairs={{0,20},{2,22},{4,16},{6,18},{16,4},{18,6},{20,0},{22,2},{1,21},{3,... | collective-permute-start | bytes 589832 | tf_op jit(solution)/shard_map/ppermute | solution.py:392
  34.0 12.0 %collective-permute-start.6 = (bf16[128,768]{1,0:T(8,128)(2,1)S(1)}, bf16[128,768]{1,0:T(8,128)(2,1)S(1)}, u32[]{:S(2)}, u32[]{:S(2)}) collective-permute-start(bf16[128,768]{1,0:T(8,128)(2,1)S(1)} %dynamic-slice_bitcast_fusion.1), channel_id=1, source_target_pairs={{0,22},{2,16},{4,18},{6,20},{16,6},{18,0},{20,2},{22,4},{1,23},{3,... | collective-permute-start | bytes 589832 | tf_op jit(solution)/shard_map/ppermute | solution.py:392
  48.2 15.3 %collective-permute-start.7 = (bf16[384,1024]{1,0:T(8,128)(2,1)S(1)}, bf16[384,1024]{1,0:T(8,128)(2,1)S(1)}, u32[]{:S(2)}, u32[]{:S(2)}) collective-permute-start(bf16[384,1024]{1,0:T(8,128)(2,1)S(1)} %convolution_convert_fusion.1.refs_0_), channel_id=1, source_target_pairs={{0,8},{8,0},{1,9},{9,1},{2,10},{10,2},{3,11},{11,3},{4,12},{12,4},... | collective-permute-start | bytes 2359304 | tf_op jit(solution)/shard_map/ppermute | solution.py:263
  84.2 33.1 %copy-start.8 = (bf16[768,768]{1,0:T(8,128)(2,1)S(1)}, bf16[768,768]{1,0:T(8,128)(2,1)}, u32[]{:S(2)}) copy-start(bf16[768,768]{1,0:T(8,128)(2,1)} %param.17) | copy-start | bytes 3538948
  84.2 32.1 %all-to-all-start = ((bf16[8,192,128]{2,1,0:T(8,128)(2,1)}), bf16[8,192,128]{2,1,0:T(8,128)(2,1)}, u32[]{:S(2)}, u32[]{:S(2)}) async-start(bf16[8,192,128]{2,1,0:T(8,128)(2,1)} %get-tuple-element.31), calls=%async_computation | async-start | bytes 786432 | tf_op jit(solution)/shard_map/all_to_all | solution.py:337
  91.7 49.8 %collective-permute-start.8 = (bf16[320,768]{1,0:T(8,128)(2,1)}, bf16[320,768]{1,0:T(8,128)(2,1)}, u32[]{:S(2)}, u32[]{:S(2)}) collective-permute-start(bf16[320,768]{1,0:T(8,128)(2,1)} %bitcast.30), channel_id=1, source_target_pairs={{0,2},{2,4},{4,6},{6,0},{1,3},{3,5},{5,7},{7,1},{8,10},{10,12},{12... | collective-permute-start | bytes 1474568 | tf_op jit(solution)/shard_map/ppermute | solution.py:263
  93.8 79.4 %collective-permute-start.14 = (bf16[320,768]{1,0:T(8,128)(2,1)}, bf16[320,768]{1,0:T(8,128)(2,1)}, u32[]{:S(2)}, u32[]{:S(2)}) collective-permute-start(bf16[320,768]{1,0:T(8,128)(2,1)} %bitcast.30), channel_id=1, source_target_pairs={{0,6},{2,0},{4,2},{6,4},{1,7},{3,1},{5,3},{7,5},{8,14},{10,8},{12,... | collective-permute-start | bytes 1474568 | tf_op jit(solution)/shard_map/ppermute | solution.py:263
  95.7 72.4 %collective-permute-start.11 = (bf16[320,768]{1,0:T(8,128)(2,1)}, bf16[320,768]{1,0:T(8,128)(2,1)}, u32[]{:S(2)}, u32[]{:S(2)}) collective-permute-start(bf16[320,768]{1,0:T(8,128)(2,1)} %bitcast.30), channel_id=1, source_target_pairs={{0,4},{2,6},{4,0},{6,2},{1,5},{3,7},{5,1},{7,3},{8,12},{10,14},{12... | collective-permute-start | bytes 1474568 | tf_op jit(solution)/shard_map/ppermute | solution.py:263
  120.9 137.8 %copy-start.6 = (f32[256,768]{1,0:T(8,128)}, f32[256,768]{1,0:T(8,128)S(1)}, u32[]{:S(2)}) copy-start(f32[256,768]{1,0:T(8,128)S(1)} %get-tuple-element.97) | copy-start | bytes 2359300
  125.6 13.6 %all-to-all-start.1 = ((bf16[4,80,896]{2,1,0:T(8,128)(2,1)}), bf16[4,80,896]{2,1,0:T(8,128)(2,1)}, u32[]{:S(2)}, u32[]{:S(2)}) async-start(bf16[4,80,896]{2,1,0:T(8,128)(2,1)} %bitcast.282), calls=%async_computation.1 | async-start | bytes 1146880 | tf_op jit(solution)/shard_map/all_to_all | solution.py:337
  140.2 31.4 %copy-start.42 = (bf16[320,768]{1,0:T(8,128)(2,1)}, bf16[320,768]{1,0:T(8,128)(2,1)S(1)}, u32[]{:S(2)}) copy-start(bf16[320,768]{1,0:T(8,128)(2,1)S(1)} %slice.192) | copy-start | bytes 1474564
  140.3 37.0 %collective-permute-start.9 = (bf16[320,768]{1,0:T(8,128)(2,1)S(1)}, bf16[320,768]{1,0:T(8,128)(2,1)S(1)}, u32[]{:S(2)}, u32[]{:S(2)}) collective-permute-start(bf16[320,768]{1,0:T(8,128)(2,1)S(1)} %slice.192), channel_id=1, source_target_pairs={{0,2},{2,4},{4,6},{6,0},{1,3},{3,5},{5,7},{7,1},{8,10},{10,12},{12... | collective-permute-start | bytes 1474568 | tf_op jit(solution)/shard_map/ppermute | solution.py:263
  140.3 38.2 %collective-permute-start.12 = (bf16[320,768]{1,0:T(8,128)(2,1)S(1)}, bf16[320,768]{1,0:T(8,128)(2,1)S(1)}, u32[]{:S(2)}, u32[]{:S(2)}) collective-permute-start(bf16[320,768]{1,0:T(8,128)(2,1)S(1)} %slice.192), channel_id=1, source_target_pairs={{0,4},{2,6},{4,0},{6,2},{1,5},{3,7},{5,1},{7,3},{8,12},{10,14},{12... | collective-permute-start | bytes 1474568 | tf_op jit(solution)/shard_map/ppermute | solution.py:263
  141.6 39.1 %collective-permute-start.15 = (bf16[320,768]{1,0:T(8,128)(2,1)S(1)}, bf16[320,768]{1,0:T(8,128)(2,1)S(1)}, u32[]{:S(2)}, u32[]{:S(2)}) collective-permute-start(bf16[320,768]{1,0:T(8,128)(2,1)S(1)} %slice.192), channel_id=1, source_target_pairs={{0,6},{2,0},{4,2},{6,4},{1,7},{3,1},{5,3},{7,5},{8,14},{10,8},{12,... | collective-permute-start | bytes 1474568 | tf_op jit(solution)/shard_map/ppermute | solution.py:263
  175.3 62.4 %copy-start.80 = (bf16[320,768]{1,0:T(8,128)(2,1)}, bf16[320,768]{1,0:T(8,128)(2,1)S(1)}, u32[]{:S(2)}) copy-start(bf16[320,768]{1,0:T(8,128)(2,1)S(1)} %get-tuple-element.117) | copy-start | bytes 1474564
  178.5 18.0 %collective-permute-start.17 = (f32[8,320]{1,0:T(8,128)S(1)}, f32[8,320]{1,0:T(8,128)S(1)}, u32[]{:S(2)}, u32[]{:S(2)}) collective-permute-start(f32[8,320]{1,0:T(8,128)S(1)} %fusion.87), channel_id=1, source_target_pairs={{0,6},{2,0},{4,2},{6,4},{1,7},{3,1},{5,3},{7,5},{8,14},{10,8},{12,... | collective-permute-start | bytes 30728 | tf_op jit(solution)/shard_map/ppermute | solution.py:263
  179.8 17.4 %collective-permute-start.18 = (f32[8,320]{1,0:T(8,128)S(1)}, f32[8,320]{1,0:T(8,128)S(1)}, u32[]{:S(2)}, u32[]{:S(2)}) collective-permute-start(f32[8,320]{1,0:T(8,128)S(1)} %fusion.88), channel_id=1, source_target_pairs={{0,4},{2,6},{4,0},{6,2},{1,5},{3,7},{5,1},{7,3},{8,12},{10,14},{12... | collective-permute-start | bytes 30728 | tf_op jit(solution)/shard_map/ppermute | solution.py:263
  181.9 15.2 %collective-permute-start.19 = (f32[8,320]{1,0:T(8,128)S(1)}, f32[8,320]{1,0:T(8,128)S(1)}, u32[]{:S(2)}, u32[]{:S(2)}) collective-permute-start(f32[8,320]{1,0:T(8,128)S(1)} %fusion.89), channel_id=1, source_target_pairs={{0,2},{2,4},{4,6},{6,0},{1,3},{3,5},{5,7},{7,1},{8,10},{10,12},{12... | collective-permute-start | bytes 30728 | tf_op jit(solution)/shard_map/ppermute | solution.py:263
  193.7 13.2 %collective-permute-start.10 = (bf16[320,768]{1,0:T(8,128)(2,1)S(1)}, bf16[320,768]{1,0:T(8,128)(2,1)S(1)}, u32[]{:S(2)}, u32[]{:S(2)}) collective-permute-start(bf16[320,768]{1,0:T(8,128)(2,1)S(1)} %convolution_convert_fusion.10), channel_id=1, source_target_pairs={{0,6},{2,0},{4,2},{6,4},{1,7},{3,1},{5,3},{7,5},{8,14},{10,8},{12,... | collective-permute-start | bytes 1474568 | tf_op jit(solution)/shard_map/ppermute | solution.py:263
  194.4 43.3 %collective-permute-start.13 = (bf16[320,768]{1,0:T(8,128)(2,1)S(1)}, bf16[320,768]{1,0:T(8,128)(2,1)S(1)}, u32[]{:S(2)}, u32[]{:S(2)}) collective-permute-start(bf16[320,768]{1,0:T(8,128)(2,1)S(1)} %convolution_convert_fusion.9), channel_id=1, source_target_pairs={{0,4},{2,6},{4,0},{6,2},{1,5},{3,7},{5,1},{7,3},{8,12},{10,14},{12... | collective-permute-start | bytes 1474568 | tf_op jit(solution)/shard_map/ppermute | solution.py:263
  196.5 41.2 %collective-permute-start.16 = (bf16[320,768]{1,0:T(8,128)(2,1)S(1)}, bf16[320,768]{1,0:T(8,128)(2,1)S(1)}, u32[]{:S(2)}, u32[]{:S(2)}) collective-permute-start(bf16[320,768]{1,0:T(8,128)(2,1)S(1)} %convolution_convert_fusion.8), channel_id=1, source_target_pairs={{0,2},{2,4},{4,6},{6,0},{1,3},{3,5},{5,7},{7,1},{8,10},{10,12},{12... | collective-permute-start | bytes 1474568 | tf_op jit(solution)/shard_map/ppermute | solution.py:263
  238.4 15.7 %collective-permute-start.43 = (bf16[320,128]{1,0:T(8,128)(2,1)S(1)}, bf16[320,128]{1,0:T(8,128)(2,1)S(1)}, u32[]{:S(2)}, u32[]{:S(2)}) collective-permute-start(bf16[320,128]{1,0:T(8,128)(2,1)S(1)} %slice.213), channel_id=1, source_target_pairs={{0,2},{2,4},{4,6},{6,0},{1,3},{3,5},{5,7},{7,1},{8,10},{10,12},{12... | collective-permute-start | bytes 245768 | tf_op jit(solution)/shard_map/ppermute | solution.py:263
  238.5 15.6 %collective-permute-start.44 = (bf16[320,128]{1,0:T(8,128)(2,1)S(1)}, bf16[320,128]{1,0:T(8,128)(2,1)}, u32[]{:S(2)}, u32[]{:S(2)}) collective-permute-start(bf16[320,128]{1,0:T(8,128)(2,1)S(1)} %slice.213), channel_id=1, source_target_pairs={{0,4},{2,6},{4,0},{6,2},{1,5},{3,7},{5,1},{7,3},{8,12},{10,14},{12... | collective-permute-start | bytes 245768 | tf_op jit(solution)/shard_map/ppermute | solution.py:263
  240.2 13.9 %collective-permute-start.45 = (bf16[320,128]{1,0:T(8,128)(2,1)S(1)}, bf16[320,128]{1,0:T(8,128)(2,1)}, u32[]{:S(2)}, u32[]{:S(2)}) collective-permute-start(bf16[320,128]{1,0:T(8,128)(2,1)S(1)} %slice.213), channel_id=1, source_target_pairs={{0,6},{2,0},{4,2},{6,4},{1,7},{3,1},{5,3},{7,5},{8,14},{10,8},{12,... | collective-permute-start | bytes 245768 | tf_op jit(solution)/shard_map/ppermute | solution.py:263
  243.9 13.0 %all-to-all-start.3 = ((bf16[4,80,896]{2,1,0:T(8,128)(2,1)}), bf16[4,80,896]{2,1,0:T(8,128)(2,1)S(1)}, u32[]{:S(2)}, u32[]{:S(2)}) async-start(bf16[4,80,896]{2,1,0:T(8,128)(2,1)} %bitcast.259), calls=%async_computation.3 | async-start | bytes 1146880 | tf_op jit(solution)/shard_map/all_to_all | solution.py:337
  251.4 113.4 %collective-permute-start.21 = (bf16[320,768]{1,0:T(8,128)(2,1)}, bf16[320,768]{1,0:T(8,128)(2,1)}, u32[]{:S(2)}, u32[]{:S(2)}) collective-permute-start(bf16[320,768]{1,0:T(8,128)(2,1)} %convolution_convert_fusion.5), channel_id=1, source_target_pairs={{0,4},{2,6},{4,0},{6,2},{1,5},{3,7},{5,1},{7,3},{8,12},{10,14},{12... | collective-permute-start | bytes 1474568 | tf_op jit(solution)/shard_map/ppermute | solution.py:263
  262.2 23.3 %all-to-all-start.4 = ((bf16[8,192,128]{2,1,0:T(8,128)(2,1)}), bf16[8,192,128]{2,1,0:T(8,128)(2,1)S(1)}, u32[]{:S(2)}, u32[]{:S(2)}) async-start(bf16[8,192,128]{2,1,0:T(8,128)(2,1)} %bitcast.36), calls=%async_computation.4 | async-start | bytes 786432 | tf_op jit(solution)/shard_map/all_to_all | solution.py:337
  320.7 20.2 %collective-permute-start.48 = (f32[12,32]{1,0:T(8,128)}, f32[12,32]{1,0:T(8,128)}, u32[]{:S(2)}, u32[]{:S(2)}) collective-permute-start(f32[12,32]{1,0:T(8,128)} %dynamic_update_slice.5), channel_id=1, source_target_pairs={{0,8},{8,0},{1,9},{9,1},{2,10},{10,2},{3,11},{11,3},{4,12},{12,4},... | collective-permute-start | bytes 4616 | tf_op jit(solution)/shard_map/ppermute | solution.py:293
  329.1 43.3 %collective-permute-start.47 = (bf16[768,384]{1,0:T(8,128)(2,1)}, bf16[768,384]{1,0:T(8,128)(2,1)}, u32[]{:S(2)}, u32[]{:S(2)}) collective-permute-start(bf16[768,384]{1,0:T(8,128)(2,1)} %bitcast.280), channel_id=1, source_target_pairs={{0,1},{1,0},{2,3},{3,2},{4,5},{5,4},{6,7},{7,6},{8,9},{9,8},{10,11... | collective-permute-start | bytes 1769480 | tf_op jit(solution)/shard_map/ppermute | solution.py:263
  332.0 32.8 %collective-permute-start.20 = (bf16[320,768]{1,0:T(8,128)(2,1)}, bf16[320,768]{1,0:T(8,128)(2,1)}, u32[]{:S(2)}, u32[]{:S(2)}) collective-permute-start(bf16[320,768]{1,0:T(8,128)(2,1)} %convolution_convert_fusion.6), channel_id=1, source_target_pairs={{0,6},{2,0},{4,2},{6,4},{1,7},{3,1},{5,3},{7,5},{8,14},{10,8},{12,... | collective-permute-start | bytes 1474568 | tf_op jit(solution)/shard_map/ppermute | solution.py:263
  332.1 33.3 %collective-permute-start.22 = (bf16[320,768]{1,0:T(8,128)(2,1)}, bf16[320,768]{1,0:T(8,128)(2,1)}, u32[]{:S(2)}, u32[]{:S(2)}) collective-permute-start(bf16[320,768]{1,0:T(8,128)(2,1)} %convolution_convert_fusion.4), channel_id=1, source_target_pairs={{0,2},{2,4},{4,6},{6,0},{1,3},{3,5},{5,7},{7,1},{8,10},{10,12},{12... | collective-permute-start | bytes 1474568 | tf_op jit(solution)/shard_map/ppermute | solution.py:263
  342.9 3.9 collective-permute-start.49
  347.5 3.7 collective-permute-start.50
  351.1 5.2 %collective-permute-start.51 = (f32[12,32]{1,0:T(8,128)S(1)}, f32[12,32]{1,0:T(8,128)S(1)}, u32[]{:S(2)}, u32[]{:S(2)}) collective-permute-start(f32[12,32]{1,0:T(8,128)S(1)} %add.663), channel_id=1, source_target_pairs={{0,2},{2,0},{4,6},{6,4},{1,3},{3,1},{5,7},{7,5},{8,10},{10,8},{12,... | collective-permute-start | bytes 4616 | tf_op jit(solution)/shard_map/ppermute | solution.py:293
  356.3 7.2 %collective-permute-start.52 = (f32[12,32]{1,0:T(8,128)S(1)}, f32[12,32]{1,0:T(8,128)S(1)}, u32[]{:S(2)}, u32[]{:S(2)}) collective-permute-start(f32[12,32]{1,0:T(8,128)S(1)} %add.664), channel_id=1, source_target_pairs={{0,4},{2,6},{4,0},{6,2},{1,5},{3,7},{5,1},{7,3},{8,12},{10,14},{12... | collective-permute-start | bytes 4616 | tf_op jit(solution)/shard_map/ppermute | solution.py:293
  363.5 15.0 %collective-permute-start.46 = (bf16[768,384]{1,0:T(8,128)(2,1)}, bf16[768,384]{1,0:T(8,128)(2,1)}, u32[]{:S(2)}, u32[]{:S(2)}) collective-permute-start(bf16[768,384]{1,0:T(8,128)(2,1)} %bitcast.281), channel_id=1, source_target_pairs={{0,1},{1,0},{2,3},{3,2},{4,5},{5,4},{6,7},{7,6},{8,9},{9,8},{10,11... | collective-permute-start | bytes 1769480 | tf_op jit(solution)/shard_map/ppermute | solution.py:263
  364.8 15.9 %collective-permute-start.37 = (bf16[2,192,896]{2,1,0:T(8,128)(2,1)}, bf16[2,192,896]{2,1,0:T(8,128)(2,1)}, u32[]{:S(2)}, u32[]{:S(2)}) collective-permute-start(bf16[2,192,896]{2,1,0:T(8,128)(2,1)} %fusion.80), channel_id=1, source_target_pairs={{0,8},{8,0},{1,9},{9,1},{2,10},{10,2},{3,11},{11,3},{4,12},{12,4},... | collective-permute-start | bytes 2064392 | tf_op jit(solution)/shard_map/ppermute | solution.py:263
  364.8 17.9 %collective-permute-start.23 = (bf16[384,1024]{1,0:T(8,128)(2,1)S(1)}, bf16[384,1024]{1,0:T(8,128)(2,1)}, u32[]{:S(2)}, u32[]{:S(2)}) collective-permute-start(bf16[384,1024]{1,0:T(8,128)(2,1)S(1)} %get-tuple-element.47), channel_id=1, source_target_pairs={{0,8},{8,0},{1,9},{9,1},{2,10},{10,2},{3,11},{11,3},{4,12},{12,4},... | collective-permute-start | bytes 2359304 | tf_op jit(solution)/shard_map/ppermute | solution.py:263
  368.2 45.3 %all-to-all-start.5 = ((bf16[4,80,768]{2,1,0:T(8,128)(2,1)}), bf16[4,80,768]{2,1,0:T(8,128)(2,1)}, u32[]{:S(2)}, u32[]{:S(2)}) async-start(bf16[4,80,768]{2,1,0:T(8,128)(2,1)} %bitcast.283), calls=%async_computation.5 | async-start | bytes 983040 | tf_op jit(solution)/shard_map/all_to_all | solution.py:337
  386.6 10.7 %collective-permute-start.24 = (bf16[128,768]{1,0:T(8,128)(2,1)S(1)}, bf16[128,768]{1,0:T(8,128)(2,1)S(1)}, u32[]{:S(2)}, u32[]{:S(2)}) collective-permute-start(bf16[128,768]{1,0:T(8,128)(2,1)S(1)} %get-tuple-element.115), channel_id=1, source_target_pairs={{2,0},{4,2},{6,4},{0,6},{18,16},{20,18},{22,20},{16,22},{3,1},{5,3... | collective-permute-start | bytes 589832 | tf_op jit(solution)/shard_map/ppermute | solution.py:600
  389.3 24.3 %collective-permute-start.25 = (bf16[128,768]{1,0:T(8,128)(2,1)S(1)}, bf16[128,768]{1,0:T(8,128)(2,1)S(1)}, u32[]{:S(2)}, u32[]{:S(2)}) collective-permute-start(bf16[128,768]{1,0:T(8,128)(2,1)S(1)} %get-tuple-element.114), channel_id=1, source_target_pairs={{4,0},{6,2},{0,4},{2,6},{20,16},{22,18},{16,20},{18,22},{5,1},{7,3... | collective-permute-start | bytes 589832 | tf_op jit(solution)/shard_map/ppermute | solution.py:600
  391.0 24.9 %collective-permute-start.26 = (bf16[128,768]{1,0:T(8,128)(2,1)}, bf16[128,768]{1,0:T(8,128)(2,1)S(1)}, u32[]{:S(2)}, u32[]{:S(2)}) collective-permute-start(bf16[128,768]{1,0:T(8,128)(2,1)} %get-tuple-element.113), channel_id=1, source_target_pairs={{6,0},{0,2},{2,4},{4,6},{22,16},{16,18},{18,20},{20,22},{7,1},{1,3... | collective-permute-start | bytes 589832 | tf_op jit(solution)/shard_map/ppermute | solution.py:600
  393.0 24.2 %collective-permute-start.27 = (bf16[128,768]{1,0:T(8,128)(2,1)}, bf16[128,768]{1,0:T(8,128)(2,1)S(1)}, u32[]{:S(2)}, u32[]{:S(2)}) collective-permute-start(bf16[128,768]{1,0:T(8,128)(2,1)} %get-tuple-element.112), channel_id=1, source_target_pairs={{16,0},{18,2},{20,4},{22,6},{0,16},{2,18},{4,20},{6,22},{17,1},{19... | collective-permute-start | bytes 589832 | tf_op jit(solution)/shard_map/ppermute | solution.py:600
  393.7 23.5 %collective-permute-start.28 = (bf16[128,768]{1,0:T(8,128)(2,1)}, bf16[128,768]{1,0:T(8,128)(2,1)S(1)}, u32[]{:S(2)}, u32[]{:S(2)}) collective-permute-start(bf16[128,768]{1,0:T(8,128)(2,1)} %get-tuple-element.111), channel_id=1, source_target_pairs={{18,0},{20,2},{22,4},{16,6},{2,16},{4,18},{6,20},{0,22},{19,1},{21... | collective-permute-start | bytes 589832 | tf_op jit(solution)/shard_map/ppermute | solution.py:600
  397.3 25.6 %collective-permute-start.29 = (bf16[128,768]{1,0:T(8,128)(2,1)}, bf16[128,768]{1,0:T(8,128)(2,1)S(1)}, u32[]{:S(2)}, u32[]{:S(2)}) collective-permute-start(bf16[128,768]{1,0:T(8,128)(2,1)} %get-tuple-element.110), channel_id=1, source_target_pairs={{20,0},{22,2},{16,4},{18,6},{4,16},{6,18},{0,20},{2,22},{21,1},{23... | collective-permute-start | bytes 589832 | tf_op jit(solution)/shard_map/ppermute | solution.py:600
  413.6 9.3 %collective-permute-start.30 = (bf16[128,768]{1,0:T(8,128)(2,1)}, bf16[128,768]{1,0:T(8,128)(2,1)S(1)}, u32[]{:S(2)}, u32[]{:S(2)}) collective-permute-start(bf16[128,768]{1,0:T(8,128)(2,1)} %get-tuple-element.109), channel_id=1, source_target_pairs={{22,0},{16,2},{18,4},{20,6},{6,16},{0,18},{2,20},{4,22},{23,1},{17... | collective-permute-start | bytes 589832 | tf_op jit(solution)/shard_map/ppermute | solution.py:600
  415.9 11.3 %collective-permute-start.38 = (bf16[192,896]{1,0:T(8,128)(2,1)S(1)}, bf16[192,896]{1,0:T(8,128)(2,1)S(1)}, u32[]{:S(2)}, u32[]{:S(2)}) collective-permute-start(bf16[192,896]{1,0:T(8,128)(2,1)S(1)} %copy-done.49), channel_id=1, source_target_pairs={{0,16},{16,0},{1,17},{17,1},{2,18},{18,2},{3,19},{19,3},{4,20},{20... | collective-permute-start | bytes 1032200 | tf_op jit(solution)/shard_map/ppermute | solution.py:263
  417.2 22.1 %collective-permute-start.31 = (bf16[2,192,576]{2,1,0:T(8,128)(2,1)S(1)}, bf16[2,192,576]{2,1,0:T(8,128)(2,1)S(1)}, u32[]{:S(2)}, u32[]{:S(2)}) collective-permute-start(bf16[2,192,576]{2,1,0:T(8,128)(2,1)S(1)} %copy-done.39), channel_id=1, source_target_pairs={{0,8},{8,0},{1,9},{9,1},{2,10},{10,2},{3,11},{11,3},{4,12},{12,4},... | collective-permute-start | bytes 1327112 | tf_op jit(solution)/shard_map/ppermute | solution.py:263
  427.4 5.5 %collective-permute-start.39 = (bf16[4,24,896]{2,1,0:T(8,128)(2,1)S(1)}, bf16[4,24,896]{2,1,0:T(8,128)(2,1)S(1)}, u32[]{:S(2)}, u32[]{:S(2)}) collective-permute-start(bf16[4,24,896]{2,1,0:T(8,128)(2,1)S(1)} %fusion.128), channel_id=1, source_target_pairs={{0,1},{1,0},{2,3},{3,2},{4,5},{5,4},{6,7},{7,6},{8,9},{9,8},{10,11... | collective-permute-start | bytes 516104 | tf_op jit(solution)/shard_map/ppermute | solution.py:263
  432.9 7.2 %collective-permute-start.40 = (bf16[24,896]{1,0:T(8,128)(2,1)S(1)}, bf16[24,896]{1,0:T(8,128)(2,1)S(1)}, u32[]{:S(2)}, u32[]{:S(2)}) collective-permute-start(bf16[24,896]{1,0:T(8,128)(2,1)S(1)} %get-tuple-element.126), channel_id=1, source_target_pairs={{0,2},{2,4},{4,6},{6,0},{1,3},{3,5},{5,7},{7,1},{8,10},{10,12},{12... | collective-permute-start | bytes 129032 | tf_op jit(solution)/shard_map/ppermute | solution.py:263
  433.7 6.4 %collective-permute-start.41 = (bf16[24,896]{1,0:T(8,128)(2,1)S(1)}, bf16[24,896]{1,0:T(8,128)(2,1)S(1)}, u32[]{:S(2)}, u32[]{:S(2)}) collective-permute-start(bf16[24,896]{1,0:T(8,128)(2,1)S(1)} %get-tuple-element.128), channel_id=1, source_target_pairs={{0,4},{2,6},{4,0},{6,2},{1,5},{3,7},{5,1},{7,3},{8,12},{10,14},{12... | collective-permute-start | bytes 129032 | tf_op jit(solution)/shard_map/ppermute | solution.py:263
  436.4 4.5 collective-permute-start.42
  439.4 6.3 %collective-permute-start.32 = (bf16[192,576]{1,0:T(8,128)(2,1)S(1)}, bf16[192,576]{1,0:T(8,128)(2,1)S(1)}, u32[]{:S(2)}, u32[]{:S(2)}) collective-permute-start(bf16[192,576]{1,0:T(8,128)(2,1)S(1)} %fusion.121), channel_id=1, source_target_pairs={{0,16},{16,0},{1,17},{17,1},{2,18},{18,2},{3,19},{19,3},{4,20},{20... | collective-permute-start | bytes 663560 | tf_op jit(solution)/shard_map/ppermute | solution.py:263
  445.7 4.9 %collective-permute-start.33 = (bf16[4,24,576]{2,1,0:T(8,128)(2,1)S(1)}, bf16[4,24,576]{2,1,0:T(8,128)(2,1)S(1)}, u32[]{:S(2)}, u32[]{:S(2)}) collective-permute-start(bf16[4,24,576]{2,1,0:T(8,128)(2,1)S(1)} %fusion.139), channel_id=1, source_target_pairs={{0,1},{1,0},{2,3},{3,2},{4,5},{5,4},{6,7},{7,6},{8,9},{9,8},{10,11... | collective-permute-start | bytes 331784 | tf_op jit(solution)/shard_map/ppermute | solution.py:263
  450.7 3.9 collective-permute-start.36
  451.5 4.8 %collective-permute-start.35 = (bf16[24,576]{1,0:T(8,128)(2,1)S(1)}, bf16[24,576]{1,0:T(8,128)(2,1)S(1)}, u32[]{:S(2)}, u32[]{:S(2)}) collective-permute-start(bf16[24,576]{1,0:T(8,128)(2,1)S(1)} %get-tuple-element.135), channel_id=1, source_target_pairs={{0,4},{2,6},{4,0},{6,2},{1,5},{3,7},{5,1},{7,3},{8,12},{10,14},{12... | collective-permute-start | bytes 82952 | tf_op jit(solution)/shard_map/ppermute | solution.py:263
  451.5 5.8 %collective-permute-start.34 = (bf16[24,576]{1,0:T(8,128)(2,1)S(1)}, bf16[24,576]{1,0:T(8,128)(2,1)S(1)}, u32[]{:S(2)}, u32[]{:S(2)}) collective-permute-start(bf16[24,576]{1,0:T(8,128)(2,1)S(1)} %get-tuple-element.133), channel_id=1, source_target_pairs={{0,2},{2,4},{4,6},{6,0},{1,3},{3,5},{5,7},{7,1},{8,10},{10,12},{12... | collective-permute-start | bytes 82952 | tf_op jit(solution)/shard_map/ppermute | solution.py:263
  (80 other events, 475.3 us)
